TPU v7x, 32 devices: a whole 2x2x4 slice. The times are simulated.
32 devices in a mesh: dp: 4 (over y, x), mp: 8 (over z, core).
Axes of the slice: x: 2, y: 2, z: 4, core: 2. Of those that a mesh axis runs over, the one named last changes fastest.
Arguments:
- features: bfloat16 [1024, 8192], P('dp', 'mp'), may hold values from -6 to 6
- out_grads: bfloat16 [1024, 8192], P('dp', 'mp'), may hold values from -0.5 to 0.5
- matching: int32 [2, 8], P(None, 'mp'), may hold values 0 or 1
Outputs:
- blocks: bfloat16 [8192, 8192], P('dp', 'mp')
All inputs are finite; a program needn't handle non-finite values. No bound on the sum of `matching` on one device may be relied on, other than what follows from the above.
Results may differ from a plain program's by a relative error of at most 0.006.
Values may be sent and summed in bfloat16 or wider, within the bound.
A program may use at most 128 MiB of HBM per device.

v0:
```python
import jax
import jax.numpy as jnp
from jax import lax
from jax.sharding import PartitionSpec as P

ROUNDS = 2
NS_STEPS = 2


def shifted(value, axis, steps):
    count = lax.axis_size(axis)
    pairs = [(source, (source + steps) % count) for source in range(count)]
    return lax.ppermute(value, axis, pairs)


def contract_first(left, right):
    return lax.dot_general(
        left, right, (((0,), (0,)), ((), ())), preferred_element_type=jnp.float32
    )


def polar_step(mine, iterate):
    product = lax.dot_general(
        mine, iterate, (((1,), (1,)), ((), ())), preferred_element_type=jnp.float32
    ).astype(jnp.bfloat16)
    cubic = jnp.dot(product, iterate, preferred_element_type=jnp.float32)
    return (1.5 * mine.astype(jnp.float32) - 0.5 * cubic).astype(jnp.bfloat16)


def polar_factor(cross):
    width = cross.shape[0]
    scale = 0.5 * lax.rsqrt(jnp.sum(cross * cross) + 1e-06)
    zeros = jnp.zeros((width, width), jnp.float32)
    upper = jnp.concatenate([zeros, scale * cross], axis=1)
    lower = jnp.concatenate([-scale * cross.T, zeros], axis=1)
    iterate = (
        jnp.eye(2 * width, dtype=jnp.float32) + jnp.concatenate([upper, lower], axis=0)
    ).astype(jnp.bfloat16)
    for step in range(NS_STEPS):
        iterate = polar_step(iterate, iterate)
    return iterate


def on_device(features, out_grads, matching):
    width = out_grads.shape[1] // 2
    partial_terms = contract_first(lax.all_gather(features, "mp", axis=1, tiled=True), out_grads)
    grad = lax.psum_scatter(partial_terms, "dp", scatter_dimension=0, tiled=True)
    grad = grad.astype(jnp.bfloat16)
    first = grad[:, :width]
    second = grad[:, width:]
    for step in range(ROUNDS):
        cross = lax.psum(contract_first(first, second), "dp")
        rotation = polar_factor(cross)
        joined = jnp.concatenate([first, second], axis=1)
        turned = jnp.dot(joined, rotation, preferred_element_type=jnp.float32).astype(jnp.bfloat16)
        first = turned[:, :width]
        second = turned[:, width:]
        picked = matching[step, 0]
        moving = jnp.where(picked == 0, second, first)
        staying = jnp.where(picked == 0, first, second)
        second = shifted(moving, "mp", 1)
        first = staying
    return jnp.concatenate([first, second], axis=1)


def solution(mesh):
    return jax.shard_map(
        on_device,
        mesh=mesh,
        in_specs=(P("dp", "mp"), P("dp", "mp"), P(None, "mp")),
        out_specs=P("dp", "mp"),
        check_vma=False,
    )
```

profile of v0, /device:TPU:0, one launch (start us, length us, event | category | flops | bytes accessed | tf_op | source)
XLA Modules:
  0.0 607.9 jit_solution(2841581920733273062)
XLA Ops:
  6.5 0.7 all-gather.2.cloned.1.call-update
  7.3 51.5 %all-gather.2.cloned.1.call-done = bf16[256,8192]{1,0:T(8,128)(2,1)} async-done(((bf16[256,1024]{1,0:T(8,128)(2,1)}), bf16[256,8192]{1,0:T(8,128)(2,1)}) %all-gather.2.cloned.1.call-update) | async-done | bytes 4194320 | tf_op jit(solution)/shard_map/all_gather | solution.py:46
  58.8 15.4 %fusion.42 = f32[8192,1024]{1,0:T(8,128)} fusion(bf16[256,8192]{1,0:T(8,128)(2,1)} %all-gather.2.cloned.1.call-done, bf16[256,1024]{1,0:T(8,128)(2,1)S(1)} %copy-done), kind=kOutput, calls=%fused_computation.49 | convolution fusion | flops 4294967296 | bytes 38273024 | tf_op jit(solution)/shard_map/dot_general | solution.py:17
  74.3 287.5 %reduce-scatter.2.cloned.1.call-done = f32[2048,1024]{1,0:T(8,128)} async-done(((f32[8192,1024]{1,0:T(8,128)}), f32[2048,1024]{1,0:T(8,128)}) %reduce-scatter.2.cloned.1.call-update) | async-done | bytes 8388624 | tf_op jit(solution)/shard_map/reduce_scatter | solution.py:47
  361.8 4.0 convert_element_type.57
  365.8 2.0 copy-done.3
  367.8 2.3 fusion.9
  370.1 0.2 all-reduce.9.cloned.1.call-start
  370.4 0.6 fusion.41
  371.7 51.2 %all-reduce.7.cloned.1.call-done = f32[512,512]{1,0:T(8,128)} async-done(((f32[512,512]{1,0:T(8,128)}), f32[512,512]{1,0:T(8,128)}) %all-reduce.7.cloned.1.call-update) | async-done | bytes 1048592 | tf_op jit(solution)/shard_map/psum | solution.py:52
  422.9 2.2 multiply_reduce_fusion.1
  425.8 1.6 copy.4
  427.3 1.1 broadcast_multiply_fusion.1
  428.5 8.5 %subtract_convert_fusion.3 = bf16[1024,1024]{0,1:T(8,128)(2,1)} fusion(f32[512,512]{0,1:T(8,128)S(1)} %multiply_bitcast_fusion.1, f32[512,512]{0,1:T(8,128)} %broadcast_multiply_fusion.1), kind=kOutput, calls=%fused_computation.16 | convolution fusion | flops 4329570304 | bytes 4194304 | tf_op jit(solution)/shard_map/dot_general | solution.py:26
  437.0 8.2 %subtract_convert_fusion.2 = bf16[1024,1024]{0,1:T(8,128)(2,1)S(1)} fusion(bf16[1024,1024]{0,1:T(8,128)(2,1)} %subtract_convert_fusion.3), kind=kOutput, calls=%fused_computation.15 | convolution fusion | flops 4301258752 | bytes 4194304 | tf_op jit(solution)/shard_map/dot_general | solution.py:26
  445.2 7.0 %convolution_convert_fusion = bf16[2048,1024]{0,1:T(8,128)(2,1)S(1)} fusion(bf16[2048,1024]{1,0:T(8,128)(2,1)} %copy-done.3, bf16[1024,1024]{0,1:T(8,128)(2,1)S(1)} %subtract_convert_fusion.2), kind=kOutput, calls=%fused_computation.19 | convolution fusion | flops 4297064448 | bytes 10485760 | tf_op jit(solution)/shard_map/dot_general | solution.py:55
  452.2 0.3 broadcast_select_fusion
  452.5 0.3 collective-permute-start
  452.8 27.2 %collective-permute-done = bf16[2048,512]{0,1:T(8,128)(2,1)S(1)} collective-permute-done((bf16[2048,512]{0,1:T(8,128)(2,1)S(1)}, bf16[2048,512]{0,1:T(8,128)(2,1)S(1)}, u32[]{:S(2)}, u32[]{:S(2)}) %collective-permute-start) | collective-permute-done | bytes 2097184 | tf_op jit(solution)/shard_map/ppermute | solution.py:13
  480.0 1.3 copy-done.7
  481.3 2.3 fusion.43
  484.3 50.3 %all-reduce.9.cloned.1.call-done = f32[512,512]{1,0:T(8,128)} async-done(((f32[512,512]{1,0:T(8,128)}), f32[512,512]{1,0:T(8,128)}) %all-reduce.9.cloned.1.call-update) | async-done | bytes 1048592 | tf_op jit(solution)/shard_map/psum | solution.py:52
  534.6 2.1 multiply_reduce_fusion
  537.4 1.5 broadcast_multiply_fusion
  538.9 1.3 copy.11
  540.2 8.4 %subtract_convert_fusion.1 = bf16[1024,1024]{0,1:T(8,128)(2,1)} fusion(f32[512,512]{0,1:T(8,128)S(1)} %get-tuple-element.10, f32[512,512]{0,1:T(8,128)} %copy.11), kind=kOutput, calls=%fused_computation.14 | convolution fusion | flops 4329570304 | bytes 4194304 | tf_op jit(solution)/shard_map/dot_general | solution.py:26
  548.6 9.6 %subtract_convert_fusion = bf16[1024,1024]{0,1:T(8,128)(2,1)} fusion(bf16[1024,1024]{0,1:T(8,128)(2,1)} %subtract_convert_fusion.1), kind=kOutput, calls=%fused_computation.13 | convolution fusion | flops 4301258752 | bytes 4194304 | tf_op jit(solution)/shard_map/dot_general | solution.py:26
  558.1 6.7 %fusion.6 = bf16[2048,1024]{0,1:T(8,128)(2,1)S(1)} fusion(bf16[1024,1024]{0,1:T(8,128)(2,1)} %subtract_convert_fusion, bf16[2048,512]{0,1:T(8,128)(2,1)} %copy-done.7, bf16[2048,512]{0,1:T(8,128)(2,1)S(1)} %copy-done.5), kind=kOutput, calls=%fused_computation.18 | convolution fusion | flops 4305453056 | bytes 10485760 | tf_op jit(solution)/shard_map/dot_general | solution.py:55
  564.9 0.3 broadcast_select_fusion.3
  565.2 27.2 %collective-permute-done.1 = bf16[2048,512]{0,1:T(8,128)(2,1)S(1)} collective-permute-done((bf16[2048,512]{0,1:T(8,128)(2,1)S(1)}, bf16[2048,512]{0,1:T(8,128)(2,1)S(1)}, u32[]{:S(2)}, u32[]{:S(2)}) %collective-permute-start.1) | collective-permute-done | bytes 2097184 | tf_op jit(solution)/shard_map/ppermute | solution.py:13
  592.5 2.5 pad_maximum_fusion
  595.0 6.4 %copy.8 = bf16[2048,1024]{1,0:T(8,128)(2,1)} copy(bf16[2048,1024]{0,1:T(8,128)(2,1)} %pad_maximum_fusion) | data formatting | bytes 8388608 | tf_op jit(solution)/shard_map/concatenate | solution.py:63
  (22 shorter events, 0.3 us)
Async XLA Ops:
  6.5 52.3 %copy-start = (bf16[256,1024]{1,0:T(8,128)(2,1)S(1)}, bf16[256,1024]{1,0:T(8,128)(2,1)}, u32[]{:S(2)}) copy-start(bf16[256,1024]{1,0:T(8,128)(2,1)} %param.4) | copy-start | bytes 1572868
  6.5 52.3 %all-gather.2.cloned.1.call-start = ((), (), s32[]{:S(2)}) async-start(), calls=%async_computation.1 | async-start | bytes 4718592 | tf_op jit(solution)/shard_map/all_gather | solution.py:46
  7.3 354.5 %reduce-scatter.2.cloned.1.call-start = ((), (), s32[]{:S(2)}) async-start(), calls=%async_computation.2 | async-start | bytes 41943040 | tf_op jit(solution)/shard_map/reduce_scatter | solution.py:47
  74.2 348.6 %all-reduce.7.cloned.1.call-start = ((), (), s32[]{:S(2)}) async-start(), calls=%async_computation.3 | async-start | bytes 2097152 | tf_op jit(solution)/shard_map/psum | solution.py:52
  365.8 2.0 copy-start.3
  367.8 2.5 copy-start.6
  370.1 164.5 %all-reduce.9.cloned.1.call-start = ((), (), s32[]{:S(2)}) async-start(), calls=%async_computation.4 | async-start | bytes 2097152 | tf_op jit(solution)/shard_map/psum | solution.py:52
  422.9 5.5 copy-start.2
  452.5 27.5 %copy-start.4 = (bf16[2048,512]{0,1:T(8,128)(2,1)}, bf16[2048,512]{0,1:T(8,128)(2,1)S(1)}, u32[]{:S(2)}) copy-start(bf16[2048,512]{0,1:T(8,128)(2,1)S(1)} %get-tuple-element.8) | copy-start | bytes 6291460
  452.5 27.5 %collective-permute-start = (bf16[2048,512]{0,1:T(8,128)(2,1)S(1)}, bf16[2048,512]{0,1:T(8,128)(2,1)S(1)}, u32[]{:S(2)}, u32[]{:S(2)}) collective-permute-start(bf16[2048,512]{0,1:T(8,128)(2,1)S(1)} %get-tuple-element.7), channel_id=1, source_target_pairs={{0,1},{1,2},{2,3},{3,4},{4,5},{5,6},{6,7},{7,0},{8,9},{9,10},{10,1... | collective-permute-start | bytes 6291464 | tf_op jit(solution)/shard_map/ppermute | solution.py:13
  480.0 1.3 copy-start.7
  548.6 9.6 %copy-start.5 = (bf16[2048,512]{0,1:T(8,128)(2,1)S(1)}, bf16[2048,512]{0,1:T(8,128)(2,1)}, u32[]{:S(2)}) copy-start(bf16[2048,512]{0,1:T(8,128)(2,1)} %copy-done.4) | copy-start | bytes 6291460
  565.2 27.3 %collective-permute-start.1 = (bf16[2048,512]{0,1:T(8,128)(2,1)S(1)}, bf16[2048,512]{0,1:T(8,128)(2,1)S(1)}, u32[]{:S(2)}, u32[]{:S(2)}) collective-permute-start(bf16[2048,512]{0,1:T(8,128)(2,1)S(1)} %get-tuple-element.6), channel_id=1, source_target_pairs={{0,1},{1,2},{2,3},{3,4},{4,5},{5,6},{6,7},{7,0},{8,9},{9,10},{10,1... | collective-permute-start | bytes 6291464 | tf_op jit(solution)/shard_map/ppermute | solution.py:13
  592.5 8.9 %copy-start.1 = (bf16[256,1024]{1,0:T(8,128)(2,1)S(1)}, bf16[256,1024]{1,0:T(8,128)(2,1)}, u32[]{:S(2)}) copy-start(bf16[256,1024]{1,0:T(8,128)(2,1)} %param.4) | copy-start | bytes 1572868
Sparse Core Ops, SparseCore 0:
  9.0 49.8 all-gather.1
  74.4 287.3 reduce-scatter.1
  370.3 52.5 all-reduce.6
  483.8 50.7 all-reduce.8
where the time goes:
time: 608 us
  waiting for transfers between devices  496 us (82%)
  matrix products  68.3 us (11%)
  between operations  15.9 us (3%)
  other arithmetic  14.1 us (2%)
  local copies, waits for them, and re-layouts  13.3 us (2%)
    reduce_scatter x1, waiting for transfers between devices, on_device(): lax.psum_scatter(partial_terms, 'dp', scatter_dimension=0, tiled=True)  287 us
    psum x2, waiting for transfers between devices, on_device(): cross = lax.psum(contract_first(first, second), 'dp')  101 us
    ppermute x2, waiting for transfers between devices, shifted(): return lax.ppermute(value, axis, pairs)  54.5 us
    all_gather x1, waiting for transfers between devices, on_device(): lax.all_gather(features, 'mp', axis=1, tiled=True)  51.5 us
    dot_general x4, matrix products, polar_step(): cubic = jnp.dot(product, iterate, preferred_element_type=jnp.float32)  34.6 us
    dot_general x3, matrix products, contract_first(): lax.dot_general(left, right, (((0,), (0,)), ((), ())), preferred_element_...  20 us
    dot_general x2, matrix products, on_device(): jnp.dot(joined, rotation, preferred_element_type=jnp.float32)  13.7 us
  transfers between devices with their start and end apart: 6, of which 6 were waited for; matrix products, arithmetic and copies ran while one was open for 0% of the time, Pallas kernels for 0%

commit v1 on v0

v1 whole, which is shorter than its diff:
```python
import jax
import jax.numpy as jnp
from jax import lax
from jax.sharding import PartitionSpec as P

ROUNDS = 2


def shifted(value, axis, steps):
    count = lax.axis_size(axis)
    pairs = [(source, (source + steps) % count) for source in range(count)]
    return lax.ppermute(value, axis, pairs)


def dot(left, right, left_dim=1, right_dim=0):
    return lax.dot_general(
        left, right, (((left_dim,), (right_dim,)), ((), ())), preferred_element_type=jnp.float32
    )


def low(value):
    return value.astype(jnp.bfloat16)


def even_part(square):
    width = square.shape[0]
    half = low(square)
    second = dot(half, half)
    tail = 0.375 * jnp.eye(width, dtype=jnp.float32) - 0.3125 * square + 0.0625 * second
    return -0.5 * square + dot(low(second), low(tail))


def rotation_less_one(cross):
    scale = 0.5 * lax.rsqrt(jnp.sum(cross * cross) + 1e-06)
    angle = low(scale * cross)
    upper = even_part(dot(angle, angle, 1, 1))
    lower = even_part(dot(angle, angle, 0, 0))
    upper = low(upper)
    side = low(angle.astype(jnp.float32) + dot(upper, angle))
    return jnp.concatenate(
        [
            jnp.concatenate([upper, side], axis=1),
            jnp.concatenate([-side.T, low(lower)], axis=1),
        ],
        axis=0,
    )


def on_device(features, out_grads, matching):
    width = out_grads.shape[1] // 2
    column = lax.all_gather(features, "dp", axis=0, tiled=True)
    joined = lax.all_gather(out_grads, "dp", axis=0, tiled=True)
    wide = lax.all_gather(features, "mp", axis=1, tiled=True)
    rows = lax.all_to_all(wide, "dp", split_axis=1, concat_axis=0, tiled=True)
    slab = lax.psum_scatter(dot(features, column, 1, 1), "mp", scatter_dimension=0, tiled=True)
    gram = lax.all_gather(low(slab), ("dp", "mp"), axis=0, tiled=True)
    for step in range(ROUNDS):
        first = joined[:, :width]
        second = joined[:, width:]
        cross = dot(first, low(dot(gram, second)), 0, 0)
        turned = low(joined.astype(jnp.float32) + dot(joined, rotation_less_one(cross)))
        first = turned[:, :width]
        second = turned[:, width:]
        picked = matching[step, 0]
        moving = jnp.where(picked == 0, second, first)
        staying = jnp.where(picked == 0, first, second)
        arrived = shifted(moving, "mp", 1)
        joined = jnp.concatenate([staying, arrived], axis=1)
    return low(dot(rows, joined, 0, 0))


def solution(mesh):
    return jax.shard_map(
        on_device,
        mesh=mesh,
        in_specs=(P("dp", "mp"), P("dp", "mp"), P(None, "mp")),
        out_specs=P("dp", "mp"),
        check_vma=False,
    )
```

time: 608 us -> 315 us (0.52)
  waiting for transfers between devices: 496 us -> 217 us
  matrix products: 68.3 us -> 39.2 us
  local copies, waits for them, and re-layouts: 13.3 us -> 32.2 us
  other arithmetic: 14.1 us -> 4.08 us
    reduce_scatter x1, waiting for transfers between devices: 287 us -> 31.2 us  [on_device(): lax.psum_scatter(dot(features, column, 1, 1), 'mp', scatter_dimension=0,...]
    all_gather x1 -> x4, waiting for transfers between devices: 51.5 us -> 160 us  [the longest x1 59.4 us: on_device(): gram = lax.all_gather(low(slab), ('dp', 'mp'), axis=0, tiled=True)]
    psum x2 -> x0, waiting for transfers between devices: 101 us -> none  [on_device(): cross = lax.psum(contract_first(first, second), 'dp')]
    ppermute x2, waiting for transfers between devices: 54.5 us -> 0.01 us  [shifted(): return lax.ppermute(value, axis, pairs)]
    dot_general x9 -> x20, matrix products: 68.3 us -> 39.2 us  [dot(): lax.dot_general(left, right, (((left_dim,), (right_dim,)), ((), ())), pre...]
    all_to_all x0 -> x1, waiting for transfers between devices: none -> 25.4 us  [on_device(): rows = lax.all_to_all(wide, 'dp', split_axis=1, concat_axis=0, tiled=True)]
    dot_general x0 -> x9, local copies, waits for them, and re-layouts: none -> 12.1 us  [dot(): lax.dot_general(left, right, (((left_dim,), (right_dim,)), ((), ())), pre...]
    convert_element_type x0 -> x2, local copies, waits for them, and re-layouts: none -> 7.57 us  [the longest x1 6.39 us: low(): return value.astype(jnp.bfloat16)]
  transfers between devices with their start and end apart: 6 -> 8, of which waited for: 6 -> 6; matrix products, arithmetic and copies ran while one was open for 0% -> 17% of each run, Pallas kernels for 0% -> 0%
where the time goes in v1:
time: 315 us; the launch traced here: 314 us
  waiting for transfers between devices  217 us (69%)
  matrix products  39.2 us (12%)
  local copies, waits for them, and re-layouts  32.2 us (10%)
  between operations  16.1 us (5%)
  starting transfers between devices  5.74 us (2%)
  other arithmetic  4.08 us (1%)
    all_gather x1, waiting for transfers between devices, on_device(): gram = lax.all_gather(low(slab), ('dp', 'mp'), axis=0, tiled=True)  59.4 us
    all_gather x1, waiting for transfers between devices, on_device(): column = lax.all_gather(features, 'dp', axis=0, tiled=True)  39.9 us
    dot_general x20, matrix products, dot(): lax.dot_general(left, right, (((left_dim,), (right_dim,)), ((), ())), pre...  39.2 us
    all_gather x1, waiting for transfers between devices, on_device(): joined = lax.all_gather(out_grads, 'dp', axis=0, tiled=True)  31.5 us
    reduce_scatter x1, waiting for transfers between devices, on_device(): lax.psum_scatter(dot(features, column, 1, 1), 'mp', scatter_dimension=0,...  31.2 us
    all_gather x1, waiting for transfers between devices, on_device(): wide = lax.all_gather(features, 'mp', axis=1, tiled=True)  28.8 us
    all_to_all x1, waiting for transfers between devices, on_device(): rows = lax.all_to_all(wide, 'dp', split_axis=1, concat_axis=0, tiled=True)  25.4 us
    dot_general x9, local copies, waits for them, and re-layouts, dot(): lax.dot_general(left, right, (((left_dim,), (right_dim,)), ((), ())), pre...  12.1 us
  transfers between devices with their start and end apart: 8, of which 6 were waited for; matrix products, arithmetic and copies ran while one was open for 17% of the time, Pallas kernels for 0%

profile of v1, /device:TPU:0, one launch (start us, length us, event | category | flops | bytes accessed | tf_op | source)
XLA Modules:
  0.0 314.3 jit_solution(6198129608469640296)
XLA Ops:
  7.3 39.9 %all-gather.7.cloned.1.call-done = bf16[1024,1024]{1,0:T(8,128)(2,1)} async-done(((bf16[256,1024]{1,0:T(8,128)(2,1)}), bf16[1024,1024]{1,0:T(8,128)(2,1)}) %all-gather.7.cloned.1.call-update) | async-done | bytes 2097168 | tf_op jit(solution)/shard_map/all_gather | solution.py:51
  47.2 3.5 %fusion.97 = f32[256,1024]{1,0:T(8,128)} fusion(bf16[256,1024]{1,0:T(8,128)(2,1)} %param.3, bf16[1024,1024]{1,0:T(8,128)(2,1)} %all-gather.7.cloned.1.call-done), kind=kOutput, calls=%fused_computation.114 | convolution fusion | flops 536870912 | bytes 3670016 | tf_op jit(solution)/shard_map/dot_general | solution.py:16
  51.9 31.2 %reduce-scatter.2.cloned.1.call-done = f32[32,1024]{1,0:T(8,128)} async-done(((f32[256,1024]{1,0:T(8,128)}), f32[32,1024]{1,0:T(8,128)}) %reduce-scatter.2.cloned.1.call-update) | async-done | bytes 131088 | tf_op jit(solution)/shard_map/reduce_scatter | solution.py:55
  83.1 1.5 convert_element_type.114
  84.8 1.0 copy.50
  87.1 31.5 %all-gather.5.cloned.1.call-done = bf16[1024,1024]{0,1:T(8,128)(2,1)} async-done(((bf16[256,1024]{0,1:T(8,128)(2,1)}), bf16[1024,1024]{0,1:T(8,128)(2,1)}) %all-gather.5.cloned.1.call-update) | async-done | bytes 2097168 | tf_op jit(solution)/shard_map/all_gather | solution.py:52
  118.6 59.4 %all-gather.9.cloned.1.call-done = bf16[1024,1024]{1,0:T(8,128)(2,1)} async-done(((bf16[32,1024]{1,0:T(8,128)(2,1)}), bf16[1024,1024]{1,0:T(8,128)(2,1)}) %all-gather.9.cloned.1.call-update) | async-done | bytes 2097168 | tf_op jit(solution)/shard_map/all_gather | solution.py:56
  177.9 4.7 %multiply_reduce_fusion.1 = (f32[]{:T(128)}, f32[512,512]{1,0:T(8,128)S(1)}) fusion(bf16[1024,1024]{0,1:T(8,128)(2,1)} %all-gather.5.cloned.1.call-done, bf16[1024,1024]{1,0:T(8,128)(2,1)} %all-gather.9.cloned.1.call-done), kind=kOutput, calls=%fused_computation.58 | convolution fusion | flops 1611661312 | bytes 5242884 | tf_op jit(solution)/shard_map/dot_general | solution.py:16
  183.6 1.2 copy.38
  185.3 1.4 copy.35
  187.2 1.3 copy.36
  188.5 2.1 fusion.21
  190.7 1.3 fusion.40
  192.0 1.3 copy.39
  193.8 1.3 copy.40
  195.6 1.4 copy.41
  197.0 2.0 fusion.42
  201.0 2.4 fusion
  204.4 28.8 %all-gather.11.cloned.1.call-done = bf16[256,8192]{0,1:T(8,128)(2,1)} async-done(((bf16[256,1024]{0,1:T(8,128)(2,1)}), bf16[256,8192]{0,1:T(8,128)(2,1)}) %all-gather.11.cloned.1.call-update) | async-done | bytes 4194320 | tf_op jit(solution)/shard_map/all_gather | solution.py:53
  233.2 5.1 %all-to-all-start = ((bf16[256,4,2048]{0,2,1:T(8,128)(2,1)}), bf16[256,4,2048]{0,2,1:T(8,128)(2,1)}, u32[]{:S(2)}, u32[]{:S(2)}) async-start(bf16[256,4,2048]{0,2,1:T(8,128)(2,1)} %bitcast.43), calls=%async_computation.1 | async-start | bytes 8388608 | tf_op jit(solution)/shard_map/all_to_all | solution.py:54
  238.3 4.5 %multiply_reduce_fusion = (f32[]{:T(128)}, f32[512,512]{1,0:T(8,128)S(1)}) fusion(bf16[1024,512]{0,1:T(8,128)(2,1)S(1)} %get-tuple-element.8, bf16[1024,1024]{1,0:T(8,128)(2,1)} %all-gather.9.cloned.1.call-done, bf16[1024,512]{0,1:T(8,128)(2,1)S(1)} %collective-permute-done), kind=kOutput, calls=%fused_computation.55 | convolution fusion | flops 1611661312 | bytes 5242884 | tf_op jit(solution)/shard_map/dot_general | solution.py:16
  244.6 1.3 copy.43
  245.9 1.4 copy.44
  247.3 2.0 fusion.23
  252.1 1.3 copy.46
  253.9 1.4 copy.47
  255.2 2.2 fusion.25
  257.7 2.5 add_convert_fusion
  260.7 25.4 %all-to-all-done = bf16[256,4,2048]{0,2,1:T(8,128)(2,1)} async-done(((bf16[256,4,2048]{0,2,1:T(8,128)(2,1)}), bf16[256,4,2048]{0,2,1:T(8,128)(2,1)}, u32[]{:S(2)}, u32[]{:S(2)}) %all-to-all-start) | async-done | bytes 4194336 | tf_op jit(solution)/shard_map/all_to_all | solution.py:54
  286.1 6.2 %copy.51 = bf16[4,256,2048]{2,1,0:T(8,128)(2,1)} copy(bf16[4,256,2048]{1,2,0:T(8,128)(2,1)} %bitcast.7) | data formatting | bytes 8388608 | tf_op jit(solution)/shard_map/all_to_all | solution.py:54
  292.3 9.0 %convert_bitcast_fusion = bf16[2048,1024]{0,1:T(8,128)(2,1)} fusion(bf16[1024,2048]{1,0:T(8,128)(2,1)} %bitcast.44, bf16[1024,512]{0,1:T(8,128)(2,1)S(1)} %collective-permute-done.1, bf16[1024,512]{0,1:T(8,128)(2,1)S(1)} %get-tuple-element.5), kind=kOutput, calls=%fused_computation.2 | convolution fusion | flops 4301258752 | bytes 10485760 | tf_op jit(solution)/shard_map/dot_general | solution.py:16
  301.4 6.4 %copy.52 = bf16[2048,1024]{1,0:T(8,128)(2,1)} copy(bf16[2048,1024]{0,1:T(8,128)(2,1)} %convert_bitcast_fusion) | data formatting | bytes 8388608 | tf_op jit(solution)/shard_map/convert_element_type | solution.py:22
  (64 shorter events, 12.1 us)
Async XLA Ops:
  6.5 40.7 %all-gather.7.cloned.1.call-start = ((), (), s32[]{:S(2)}) async-start(), calls=%async_computation.3 | async-start | bytes 2621440 | tf_op jit(solution)/shard_map/all_gather | solution.py:51
  7.3 43.6 %copy-start.8 = (bf16[256,1024]{1,0:T(8,128)(2,1)S(1)}, bf16[256,1024]{1,0:T(8,128)(2,1)}, u32[]{:S(2)}) copy-start(bf16[256,1024]{1,0:T(8,128)(2,1)} %param.4) | copy-start | bytes 1572868
  7.3 75.9 %reduce-scatter.2.cloned.1.call-start = ((), (), s32[]{:S(2)}) async-start(), calls=%async_computation.4 | async-start | bytes 1179648 | tf_op jit(solution)/shard_map/reduce_scatter | solution.py:55
  50.7 34.0 %copy-start = (bf16[256,1024]{1,0:T(8,128)(2,1)S(1)}, bf16[256,1024]{1,0:T(8,128)(2,1)}, u32[]{:S(2)}) copy-start(bf16[256,1024]{1,0:T(8,128)(2,1)} %param.3) | copy-start | bytes 1572868
  50.7 35.1 %copy-start.12 = (s32[2,1]{0,1:T(1,128)S(1)}, s32[2,1]{0,1:T(1,128)}, u32[]{:S(2)}) copy-start(s32[2,1]{0,1:T(1,128)} %param.5) | copy-start | bytes 28
  50.8 67.8 %all-gather.5.cloned.1.call-start = ((), (), s32[]{:S(2)}) async-start(), calls=%async_computation.2 | async-start | bytes 2621440 | tf_op jit(solution)/shard_map/all_gather | solution.py:52
  51.9 126.1 %all-gather.9.cloned.1.call-start = ((), (), s32[]{:S(2)}) async-start(), calls=%async_computation.5 | async-start | bytes 2162688 | tf_op jit(solution)/shard_map/all_gather | solution.py:56
  84.7 148.5 %all-gather.11.cloned.1.call-start = ((), (), s32[]{:S(2)}) async-start(), calls=%async_computation.6 | async-start | bytes 4718592 | tf_op jit(solution)/shard_map/all_gather | solution.py:53
  182.7 1.0 copy-start.2
  188.5 2.1 copy-start.1
  197.0 2.0 copy-start.3
  197.0 2.2 copy-start.4
  199.2 1.1 copy-start.7
  199.2 1.8 copy-start.13
  203.5 34.7 %copy-start.5 = (bf16[1024,512]{0,1:T(8,128)(2,1)}, bf16[1024,512]{0,1:T(8,128)(2,1)S(1)}, u32[]{:S(2)}) copy-start(bf16[1024,512]{0,1:T(8,128)(2,1)S(1)} %get-tuple-element.8) | copy-start | bytes 3145732
  203.6 34.7 %collective-permute-start = (bf16[1024,512]{0,1:T(8,128)(2,1)S(1)}, bf16[1024,512]{0,1:T(8,128)(2,1)S(1)}, u32[]{:S(2)}, u32[]{:S(2)}) collective-permute-start(bf16[1024,512]{0,1:T(8,128)(2,1)S(1)} %get-tuple-element.7), channel_id=1, source_target_pairs={{0,1},{1,2},{2,3},{3,4},{4,5},{5,6},{6,7},{7,0},{8,9},{9,10},{10,1... | collective-permute-start | bytes 3145736 | tf_op jit(solution)/shard_map/ppermute | solution.py:12
  233.2 53.0 %all-to-all-start = ((bf16[256,4,2048]{0,2,1:T(8,128)(2,1)}), bf16[256,4,2048]{0,2,1:T(8,128)(2,1)}, u32[]{:S(2)}, u32[]{:S(2)}) async-start(bf16[256,4,2048]{0,2,1:T(8,128)(2,1)} %bitcast.43), calls=%async_computation.1 | async-start | bytes 8388608 | tf_op jit(solution)/shard_map/all_to_all | solution.py:54
  238.2 4.6 %copy-start.14 = (bf16[1024,512]{0,1:T(8,128)(2,1)}, bf16[1024,512]{0,1:T(8,128)(2,1)S(1)}, u32[]{:S(2)}) copy-start(bf16[1024,512]{0,1:T(8,128)(2,1)S(1)} %collective-permute-done) | copy-start | bytes 3145732
  249.7 0.8 copy-start.9
  255.2 2.2 copy-start.6
  255.2 2.2 copy-start.10
  255.2 2.2 copy-start.11
  255.2 2.5 copy-start.15
  260.4 31.9 %collective-permute-start.1 = (bf16[1024,512]{0,1:T(8,128)(2,1)S(1)}, bf16[1024,512]{0,1:T(8,128)(2,1)S(1)}, u32[]{:S(2)}, u32[]{:S(2)}) collective-permute-start(bf16[1024,512]{0,1:T(8,128)(2,1)S(1)} %get-tuple-element.6), channel_id=1, source_target_pairs={{0,1},{1,2},{2,3},{3,4},{4,5},{5,6},{6,7},{7,0},{8,9},{9,10},{10,1... | collective-permute-start | bytes 3145736 | tf_op jit(solution)/shard_map/ppermute | solution.py:12
Sparse Core Ops, SparseCore 0:
  9.2 38.0 all-gather.6
  50.9 32.2 reduce-scatter.1
  85.0 33.5 all-gather.4
  121.4 56.4 all-gather.8
  179.4 53.7 all-gather.10

commit v2 on v1

v2 whole, which is shorter than its diff:
```python
import functools

import jax
import jax.numpy as jnp
from jax import lax
from jax.experimental import pallas as pl
from jax.experimental.pallas import tpu as pltpu
from jax.sharding import PartitionSpec as P

ROUNDS = 2
TILE = 256
VMEM_BYTES = 44 * 1024 * 1024
MESH = pl.DeviceIdType.MESH


def shifted(value, axis, steps):
    count = lax.axis_size(axis)
    pairs = [(source, (source + steps) % count) for source in range(count)]
    return lax.ppermute(value, axis, pairs)


def dot(left, right, left_dim=1, right_dim=0):
    return lax.dot_general(
        left, right, (((left_dim,), (right_dim,)), ((), ())), preferred_element_type=jnp.float32
    )


def low(value):
    return value.astype(jnp.bfloat16)


def gram_kernel(
    n_dp, n_chips, f_ref, o_ref, all_ref, gram_ref,
    others, slab, sibling_half, out_half, chip_in,
    f_send, f_recv, o_send, o_recv, s_send, s_recv, z_send, z_recv,
    a_send, a_recv, b_send, b_recv, c_send, c_recv,
):
    tokens = f_ref.shape[0]
    half = tokens // 2
    piece = half // n_chips
    row = lax.axis_index("dp")
    owner = lax.axis_index("mp")
    chip = owner // 2
    core = owner % 2
    sibling = {"dp": row, "mp": chip * 2 + (1 - core)}
    rows = [{"dp": lax.rem(row + s, n_dp), "mp": owner} for s in range(1, n_dp)]
    chips = [{"dp": row, "mp": lax.rem(chip + s, n_chips) * 2 + core} for s in range(1, n_chips)]

    def remote(source, target, send, recv, device):
        return pltpu.make_async_remote_copy(
            src_ref=source, dst_ref=target, send_sem=send, recv_sem=recv,
            device_id=device, device_id_type=MESH,
        )

    barrier = pltpu.get_barrier_semaphore()
    for device in rows + chips + [sibling]:
        pl.semaphore_signal(barrier, inc=1, device_id=device, device_id_type=MESH)
    pl.semaphore_wait(barrier, n_dp + n_chips - 1)

    f_copies = [
        remote(f_ref, others.at[s], f_send.at[s], f_recv.at[s], rows[s]) for s in range(n_dp - 1)
    ]
    own_tokens = pl.ds(pl.multiple_of(row * tokens, tokens), tokens)
    o_copies = [
        remote(o_ref, all_ref.at[own_tokens], o_send.at[s], o_recv.at[s], rows[s])
        for s in range(n_dp - 1)
    ]
    for copy in f_copies + o_copies:
        copy.start()
    all_ref[own_tokens, :] = o_ref[...]

    slab[:, own_tokens] = dot(f_ref[...], f_ref[...], 1, 1)
    for s in range(n_dp - 1):
        source = lax.rem(row + n_dp - s - 1, n_dp)
        f_copies[s].wait_recv()
        slab[:, pl.ds(pl.multiple_of(source * tokens, tokens), tokens)] = dot(
            f_ref[...], others[s], 1, 1
        )

    theirs = pl.ds(pl.multiple_of((1 - core) * half, half), half)
    to_sibling = remote(slab.at[theirs], sibling_half, s_send, s_recv, sibling)
    to_sibling.start()
    to_sibling.wait_recv()
    mine = pl.multiple_of(core * half, half)
    out_half[...] = low(slab[pl.ds(mine, half), :] + sibling_half[...])

    z_copies = []
    for s in range(n_chips - 1):
        target = lax.rem(chip + s + 1, n_chips)
        z_copies.append(
            remote(
                out_half.at[pl.ds(pl.multiple_of(target * piece, piece), piece)],
                chip_in.at[s], z_send.at[s], z_recv.at[s], chips[s],
            )
        )
        z_copies[-1].start()
    offset = pl.multiple_of(chip * piece, piece)
    total = slab[pl.ds(pl.multiple_of(mine + offset, piece), piece), :] + sibling_half[pl.ds(offset, piece), :]
    for s in range(n_chips - 1):
        z_copies[s].wait_recv()
        total = total + chip_in[s].astype(jnp.float32)

    start = row * tokens + mine
    block = pl.ds(pl.multiple_of(start + offset, piece), piece)
    gram_ref[block, :] = low(total)
    a_copies = [
        remote(gram_ref.at[block], gram_ref.at[block], a_send.at[s], a_recv.at[s], chips[s])
        for s in range(n_chips - 1)
    ]
    for copy in a_copies:
        copy.start()
    for copy in a_copies:
        copy.wait_recv()

    strip = pl.ds(pl.multiple_of(start, half), half)
    b_copies = [
        remote(gram_ref.at[strip], gram_ref.at[strip], b_send.at[s], b_recv.at[s], rows[s])
        for s in range(n_dp - 1)
    ]
    for copy in b_copies:
        copy.start()
    c_copies = [remote(gram_ref.at[strip], gram_ref.at[strip], c_send.at[0], c_recv.at[0], sibling)]
    c_copies[0].start()
    for s in range(n_dp - 1):
        source = lax.rem(row + n_dp - s - 1, n_dp)
        b_copies[s].wait_recv()
        arrived = pl.ds(pl.multiple_of(source * tokens + mine, half), half)
        c_copies.append(
            remote(gram_ref.at[arrived], gram_ref.at[arrived], c_send.at[s + 1], c_recv.at[s + 1], sibling)
        )
        c_copies[-1].start()
    for copy in c_copies + o_copies:
        copy.wait_recv()
    for copy in f_copies + o_copies + [to_sibling] + z_copies + a_copies + b_copies + c_copies:
        copy.wait_send()


def gather_and_gram(features, out_grads, n_dp, n_mp):
    tokens, depth = features.shape
    every = n_dp * tokens
    n_chips = n_mp // 2
    half = tokens // 2
    dma = pltpu.SemaphoreType.DMA
    peers = [dma((n_dp - 1,))] * 2
    around = [dma((n_chips - 1,))] * 2
    whole = pl.BlockSpec(memory_space=pltpu.VMEM)
    return pl.pallas_call(
        functools.partial(gram_kernel, n_dp, n_chips),
        out_shape=[
            jax.ShapeDtypeStruct((every, out_grads.shape[1]), jnp.bfloat16),
            jax.ShapeDtypeStruct((every, every), jnp.bfloat16),
        ],
        in_specs=[whole, whole],
        out_specs=[whole, whole],
        scratch_shapes=[
            pltpu.VMEM((n_dp - 1, tokens, depth), jnp.bfloat16),
            pltpu.VMEM((tokens, every), jnp.float32),
            pltpu.VMEM((half, every), jnp.float32),
            pltpu.VMEM((half, every), jnp.bfloat16),
            pltpu.VMEM((n_chips - 1, half // n_chips, every), jnp.bfloat16),
        ]
        + peers + peers + [dma, dma] + around + around + peers + [dma((n_dp,))] * 2,
        compiler_params=pltpu.CompilerParams(
            collective_id=0, has_side_effects=True, vmem_limit_bytes=VMEM_BYTES
        ),
        cost_estimate=pl.CostEstimate(flops=2 * tokens * every * depth, bytes_accessed=200_000_000, transcendentals=0),
        name="gather_and_gram",
    )(features, out_grads)


def even_part(square):
    width = square.shape[0]
    half = low(square)
    second = dot(half, half)
    on_diagonal = lax.broadcasted_iota(jnp.int32, (width, width), 0) == lax.broadcasted_iota(
        jnp.int32, (width, width), 1
    )
    tail = jnp.where(on_diagonal, 0.375, 0.0) - 0.3125 * square + 0.0625 * second
    return low(-0.5 * square + dot(low(second), low(tail)))


def round_kernel(picked_ref, gram_ref, first_ref, second_ref, staying_ref, moving_ref, cross, upper, lower, side):
    tokens = gram_ref.shape[0]
    cross[...] = jnp.zeros_like(cross)

    @pl.loop(0, tokens // TILE)
    def _(step):
        tile = pl.ds(pl.multiple_of(step * TILE, TILE), TILE)
        cross[...] += dot(first_ref[tile, :], low(dot(gram_ref[tile, :], second_ref[...])), 0, 0)

    value = cross[...]
    scale = 0.5 * lax.rsqrt(jnp.sum(value * value) + 1e-06)
    angle = low(scale * value)
    upper[...] = even_part(dot(angle, angle, 1, 1))
    lower[...] = even_part(dot(angle, angle, 0, 0))
    side[...] = low(angle.astype(jnp.float32) + dot(upper[...], angle))
    keep = picked_ref[0] == 0

    @pl.loop(0, tokens // TILE)
    def _(step):
        tile = pl.ds(pl.multiple_of(step * TILE, TILE), TILE)
        first = first_ref[tile, :]
        second = second_ref[tile, :]
        new_first = low(first.astype(jnp.float32) + (dot(first, upper[...]) - dot(second, side[...], 1, 1)))
        new_second = low(second.astype(jnp.float32) + (dot(first, side[...]) + dot(second, lower[...])))
        moving_ref[tile, :] = jnp.where(keep, new_second, new_first)
        staying_ref[tile, :] = jnp.where(keep, new_first, new_second)


def one_round(picked, gram, first, second, second_at):
    tokens = gram.shape[0]
    width = second.shape[1] // (second_at + 1)
    block = jax.ShapeDtypeStruct((tokens, width), jnp.bfloat16)
    return pl.pallas_call(
        round_kernel,
        grid=(1,),
        out_shape=[block, block],
        in_specs=[
            pl.BlockSpec(memory_space=pltpu.SMEM),
            pl.BlockSpec((tokens, tokens), lambda i: (0, 0)),
            pl.BlockSpec((tokens, width), lambda i: (0, 0)),
            pl.BlockSpec((tokens, width), lambda i: (0, second_at)),
        ],
        out_specs=[pl.BlockSpec((tokens, width), lambda i: (0, 0))] * 2,
        scratch_shapes=[
            pltpu.VMEM((width, width), jnp.float32),
            pltpu.VMEM((width, width), jnp.bfloat16),
            pltpu.VMEM((width, width), jnp.bfloat16),
            pltpu.VMEM((width, width), jnp.bfloat16),
        ],
        compiler_params=pltpu.CompilerParams(vmem_limit_bytes=VMEM_BYTES),
        cost_estimate=pl.CostEstimate(
            flops=2 * tokens * width * (tokens + 5 * width) + 14 * width**3,
            bytes_accessed=2 * tokens * (tokens + 4 * width), transcendentals=1,
        ),
        name="jacobi_round",
    )(picked, gram, first, second)


def product_kernel(n_dp, tokens, *refs):
    parts = refs[:n_dp]
    staying_ref, arrived_ref, out_ref = refs[n_dp:]
    row = lax.axis_index("dp")
    width = staying_ref.shape[1]
    for side, block in enumerate((staying_ref, arrived_ref)):
        total = None
        for s in range(n_dp):
            source = lax.rem(row + n_dp - s, n_dp)
            term = dot(parts[s][0], block[pl.ds(pl.multiple_of(source * tokens, tokens), tokens), :], 0, 0)
            total = term if total is None else total + term
        out_ref[:, side * width : (side + 1) * width] = low(total)


def final_product(parts, staying, arrived):
    n_dp = len(parts)
    groups, tokens, depth = parts[0].shape
    tile = min(TILE, depth)
    per = depth // tile
    width = staying.shape[1]
    full = pl.BlockSpec(staying.shape, lambda i: (0, 0))
    return pl.pallas_call(
        functools.partial(product_kernel, n_dp, tokens),
        grid=(groups * per,),
        out_shape=jax.ShapeDtypeStruct((groups * depth, 2 * width), jnp.bfloat16),
        in_specs=[pl.BlockSpec((1, tokens, tile), lambda i: (i // per, 0, i % per))] * n_dp + [full, full],
        out_specs=pl.BlockSpec((tile, 2 * width), lambda i: (i, 0)),
        compiler_params=pltpu.CompilerParams(vmem_limit_bytes=VMEM_BYTES),
        cost_estimate=pl.CostEstimate(
            flops=4 * groups * depth * width * tokens * n_dp,
            bytes_accessed=2 * groups * depth * (n_dp * tokens + 2 * width), transcendentals=0,
        ),
        name="final_product",
    )(*parts, staying, arrived)


def on_device(features, out_grads, matching):
    n_dp = lax.axis_size("dp")
    n_mp = lax.axis_size("mp")
    groups = n_mp // n_dp
    row = lax.axis_index("dp")
    wide = lax.all_gather(features, "mp", axis=0)
    joined, gram = gather_and_gram(features, out_grads, n_dp, n_mp)
    parts = []
    for s in range(n_dp):
        target = lax.rem(row + s, n_dp)
        part = lax.dynamic_slice_in_dim(wide, target * groups, groups, axis=0)
        parts.append(shifted(part, "dp", s) if s else part)
    first, second, second_at = joined, joined, 1
    for step in range(ROUNDS):
        first, moving = one_round(matching[step], gram, first, second, second_at)
        second, second_at = shifted(moving, "mp", 1), 0
    return final_product(parts, first, second)


def solution(mesh):
    return jax.shard_map(
        on_device,
        mesh=mesh,
        in_specs=(P("dp", "mp"), P("dp", "mp"), P(None, "mp")),
        out_specs=P("dp", "mp"),
        check_vma=False,
    )
```

time: 315 us -> 188 us (0.60)
  waiting for transfers between devices: 217 us -> 65 us
  Pallas kernels: 0 us -> 96.1 us
  matrix products: 39.2 us -> 0 us
  local copies, waits for them, and re-layouts: 32.2 us -> 9.87 us
  other arithmetic: 4.08 us -> 0 us
    all_gather x4 -> x1, waiting for transfers between devices: 160 us -> 0.02 us  [on_device(): wide = lax.all_gather(features, 'mp', axis=0)]
    pallas_call x0 -> x4, Pallas kernels: none -> 96.1 us  [the longest x1 69.9 us: gather_and_gram(): pl.pallas_call(functools.partial(gram_kernel, n_dp, n_chips), out_shape=[...]
    ppermute x2 -> x5, waiting for transfers between devices: 0.01 us -> 64.2 us  [shifted(): return lax.ppermute(value, axis, pairs)]
    dot_general x20 -> x0, matrix products: 39.2 us -> none  [dot(): lax.dot_general(left, right, (((left_dim,), (right_dim,)), ((), ())), pre...]
    reduce_scatter x1 -> x0, waiting for transfers between devices: 31.2 us -> none  [on_device(): lax.psum_scatter(dot(features, column, 1, 1), 'mp', scatter_dimension=0,...]
    all_to_all x1 -> x0, waiting for transfers between devices: 25.4 us -> none  [on_device(): rows = lax.all_to_all(wide, 'dp', split_axis=1, concat_axis=0, tiled=True)]
    dot_general x9 -> x0, local copies, waits for them, and re-layouts: 12.1 us -> none  [dot(): lax.dot_general(left, right, (((left_dim,), (right_dim,)), ((), ())), pre...]
    convert_element_type x2 -> x0, local copies, waits for them, and re-layouts: 7.57 us -> none  [the longest x1 6.39 us: low(): return value.astype(jnp.bfloat16)]
  transfers between devices with their start and end apart: 8 -> 6, of which waited for: 6 -> 4; matrix products, arithmetic and copies ran while one was open for 17% -> 2% of each run, Pallas kernels for 0% -> 47%
where the time goes in v2:
time: 188 us; the launch traced here: 187 us
  Pallas kernels  96.1 us (51%)
  waiting for transfers between devices  65 us (35%)
  between operations  13.5 us (7%)
  local copies, waits for them, and re-layouts  9.87 us (5%)
  starting transfers between devices  2.9 us (2%)
    pallas_call x1, Pallas kernels, gather_and_gram(): pl.pallas_call(functools.partial(gram_kernel, n_dp, n_chips), out_shape=[...  69.9 us
    ppermute x5, waiting for transfers between devices, shifted(): return lax.ppermute(value, axis, pairs)  64.2 us
    pallas_call x2, Pallas kernels, one_round(): pl.pallas_call(round_kernel, grid=(1,), out_shape=[block, block], in_spec...  18.6 us
    pallas_call x1, Pallas kernels, final_product(): pl.pallas_call(functools.partial(product_kernel, n_dp, tokens), grid=(gro...  7.54 us
    unnamed x12, local copies, waits for them, and re-layouts  5.86 us
  transfers between devices with their start and end apart: 6, of which 4 were waited for; matrix products, arithmetic and copies ran while one was open for 2% of the time, Pallas kernels for 47%

profile of v2, /device:TPU:0, one launch (start us, length us, event | category | flops | bytes accessed | tf_op | source)
XLA Modules:
  0.0 187.3 jit_solution(18355288313997907234)
XLA Ops:
  6.5 0.0 all-gather.3.cloned.1.call-start
  6.5 0.7 all-gather.3.cloned.1.call-update
  7.3 0.0 copy-start
  7.3 1.0 copy-done
  8.3 0.0 copy-start.1
  8.3 1.0 copy-done.1
  9.3 69.9 %gather_and_gram.1 = (bf16[1024,1024]{1,0:T(8,128)(2,1)S(1)}, bf16[1024,1024]{1,0:T(8,128)(2,1)S(1)}) custom-call(bf16[256,1024]{1,0:T(8,128)(2,1)S(1)} %copy-done, bf16[256,1024]{1,0:T(8,128)(2,1)S(1)} %copy-done.1), custom_call_target="tpu_custom_call" | custom-call | flops 536870912 | bytes 200000000 | tf_op jit(solution)/shard_map/gather_and_gram/pallas_call | solution.py:147
  79.3 0.0 copy-start.2
  79.3 1.4 fusion
  80.7 9.4 %jacobi_round.2 = (bf16[1024,512]{1,0:T(8,128)(2,1)S(1)}, bf16[1024,512]{1,0:T(8,128)(2,1)S(1)}) custom-call(s32[1]{0:T(128)} %bitcast.2.picked_ref, bf16[1024,1024]{1,0:T(8,128)(2,1)S(1)} %get-tuple-element.11.gram_ref, bf16[1024,1024]{1,0:T(8,128)(2,1)S(1)} %get-tuple-element.12.first_ref.second_ref, ...), custom_call_target="tpu_custom_call" | custom-call | flops 5637144576 | bytes 6291456 | tf_op jit(solution)/shard_map/jacobi_round/pallas_call | solution.py:214
  90.1 0.0 copy-done.2
  90.1 0.0 copy-start.4
  90.1 1.0 copy-done.4
  91.0 0.2 collective-permute-start.3
  91.3 18.0 %collective-permute-done.3.second_ref = bf16[1024,512]{1,0:T(8,128)(2,1)S(1)} collective-permute-done((bf16[1024,512]{1,0:T(8,128)(2,1)S(1)}, bf16[1024,512]{1,0:T(8,128)(2,1)S(1)}, u32[]{:S(2)}, u32[]{:S(2)}) %collective-permute-start.3) | collective-permute-done | bytes 1048608 | tf_op jit(solution)/shard_map/ppermute | solution.py:19
  109.3 0.0 copy-start.3
  109.3 1.6 copy-done.3
  110.9 0.0 copy-start.5
  110.9 1.2 copy-done.5
  112.1 9.2 %jacobi_round.3 = (bf16[1024,512]{1,0:T(8,128)(2,1)S(1)}, bf16[1024,512]{1,0:T(8,128)(2,1)S(1)}) custom-call(s32[1]{0:T(128)} %bitcast.1.picked_ref, bf16[1024,1024]{1,0:T(8,128)(2,1)S(1)} %copy-done.3, bf16[1024,512]{1,0:T(8,128)(2,1)S(1)} %copy-done.5, bf16[1024,512]{1,0:T(8,128)(2,1)S(1)} %collective-permute-done.3.second_ref), custom_call_target="tpu_custom_call" | custom-call | flops 5637144576 | bytes 6291456 | tf_op jit(solution)/shard_map/jacobi_round/pallas_call | solution.py:214
  121.4 0.1 collective-permute-start.4
  121.4 0.0 all-gather.3.cloned.1.call-done
  121.5 2.6 %constant_dynamic-slice_fusion = (bf16[2,256,1024]{2,1,0:T(8,128)(2,1)S(1)}, bf16[2,256,1024]{2,1,0:T(8,128)(2,1)S(1)}, bf16[2,256,1024]{2,1,0:T(8,128)(2,1)S(1)}, bf16[2,256,1024]{2,1,0:T(8,128)(2,1)S(1)}) fusion(bf16[8,256,1024]{2,1,0:T(8,128)(2,1)} %bitcast.3, s32[]{:T(128)S(6)} %select_n.15, s32[]{:T(128)S(6)} %select_n.14, s32[]{:T(128)S(6)} %select_n.13, ...), kind=kLoop, calls=%fused_computation | loop fusion | bytes 8388624 | tf_op jit(solution)/shard_map/dynamic_slice | solution.py:286
  124.1 1.6 collective-permute-start.2
  125.7 1.0 collective-permute-start.1
  126.7 0.0 collective-permute-start
  126.7 10.7 %collective-permute-done.4.refs_5_ = bf16[1024,512]{1,0:T(8,128)(2,1)S(1)} collective-permute-done((bf16[1024,512]{1,0:T(8,128)(2,1)S(1)}, bf16[1024,512]{1,0:T(8,128)(2,1)S(1)}, u32[]{:S(2)}, u32[]{:S(2)}) %collective-permute-start.4) | collective-permute-done | bytes 1048608 | tf_op jit(solution)/shard_map/ppermute | solution.py:19
  137.4 12.7 %collective-permute-done.2.refs_3_ = bf16[2,256,1024]{2,1,0:T(8,128)(2,1)S(1)} collective-permute-done((bf16[2,256,1024]{2,1,0:T(8,128)(2,1)S(1)}, bf16[2,256,1024]{2,1,0:T(8,128)(2,1)S(1)}, u32[]{:S(2)}, u32[]{:S(2)}) %collective-permute-start.2) | collective-permute-done | bytes 1048608 | tf_op jit(solution)/shard_map/ppermute | solution.py:19
  150.1 22.8 %collective-permute-done.1.refs_2_ = bf16[2,256,1024]{2,1,0:T(8,128)(2,1)S(1)} collective-permute-done((bf16[2,256,1024]{2,1,0:T(8,128)(2,1)S(1)}, bf16[2,256,1024]{2,1,0:T(8,128)(2,1)S(1)}, u32[]{:S(2)}, u32[]{:S(2)}) %collective-permute-start.1) | collective-permute-done | bytes 1048608 | tf_op jit(solution)/shard_map/ppermute | solution.py:19
  172.9 0.0 collective-permute-done.refs_1_
  172.9 7.5 %final_product.1 = bf16[2048,1024]{1,0:T(8,128)(2,1)} custom-call(bf16[2,256,1024]{2,1,0:T(8,128)(2,1)S(1)} %get-tuple-element.20.refs_0_, bf16[2,256,1024]{2,1,0:T(8,128)(2,1)S(1)} %collective-permute-done.refs_1_, bf16[2,256,1024]{2,1,0:T(8,128)(2,1)S(1)} %collective-permute-done.1.refs_2_, bf16[2,256,1024]{2,1,0:T(8,128)(2,1)S(1)} %collective-permute-done.2.refs_3_, ...), custom_call_target="tpu_custom_call" | custom-call | flops 4294967296 | bytes 8388608 | tf_op jit(solution)/shard_map/final_product/pallas_call | solution.py:261
Async XLA Ops:
  6.5 114.9 %all-gather.3.cloned.1.call-start = ((), (), s32[]{:S(2)}) async-start(), calls=%async_computation | async-start | bytes 4718592 | tf_op jit(solution)/shard_map/all_gather | solution.py:281
  7.3 1.0 copy-start
  8.3 1.0 copy-start.1
  79.3 10.8 %copy-start.2 = (bf16[1024,1024]{1,0:T(8,128)(2,1)}, bf16[1024,1024]{1,0:T(8,128)(2,1)S(1)}, u32[]{:S(2)}) copy-start(bf16[1024,1024]{1,0:T(8,128)(2,1)S(1)} %get-tuple-element.11.gram_ref) | copy-start | bytes 6291460
  90.1 1.0 copy-start.4
  91.0 18.2 %collective-permute-start.3 = (bf16[1024,512]{1,0:T(8,128)(2,1)S(1)}, bf16[1024,512]{1,0:T(8,128)(2,1)S(1)}, u32[]{:S(2)}, u32[]{:S(2)}) collective-permute-start(bf16[1024,512]{1,0:T(8,128)(2,1)S(1)} %get-tuple-element.14), channel_id=1, source_target_pairs={{0,1},{1,2},{2,3},{3,4},{4,5},{5,6},{6,7},{7,0},{8,9},{9,10},{10,1... | collective-permute-start | bytes 3145736 | tf_op jit(solution)/shard_map/ppermute | solution.py:19
  109.3 1.6 copy-start.3
  110.9 1.2 copy-start.5
  121.4 16.1 %collective-permute-start.4 = (bf16[1024,512]{1,0:T(8,128)(2,1)S(1)}, bf16[1024,512]{1,0:T(8,128)(2,1)S(1)}, u32[]{:S(2)}, u32[]{:S(2)}) collective-permute-start(bf16[1024,512]{1,0:T(8,128)(2,1)S(1)} %get-tuple-element.16), channel_id=1, source_target_pairs={{0,1},{1,2},{2,3},{3,4},{4,5},{5,6},{6,7},{7,0},{8,9},{9,10},{10,1... | collective-permute-start | bytes 3145736 | tf_op jit(solution)/shard_map/ppermute | solution.py:19
  124.1 26.0 %collective-permute-start.2 = (bf16[2,256,1024]{2,1,0:T(8,128)(2,1)S(1)}, bf16[2,256,1024]{2,1,0:T(8,128)(2,1)S(1)}, u32[]{:S(2)}, u32[]{:S(2)}) collective-permute-start(bf16[2,256,1024]{2,1,0:T(8,128)(2,1)S(1)} %get-tuple-element.17), channel_id=1, source_target_pairs={{0,24},{8,0},{16,8},{24,16},{1,25},{9,1},{17,9},{25,17},{2,26},{10... | collective-permute-start | bytes 3145736 | tf_op jit(solution)/shard_map/ppermute | solution.py:19
  125.7 47.2 %collective-permute-start.1 = (bf16[2,256,1024]{2,1,0:T(8,128)(2,1)S(1)}, bf16[2,256,1024]{2,1,0:T(8,128)(2,1)S(1)}, u32[]{:S(2)}, u32[]{:S(2)}) collective-permute-start(bf16[2,256,1024]{2,1,0:T(8,128)(2,1)S(1)} %get-tuple-element.18), channel_id=1, source_target_pairs={{0,16},{8,24},{16,0},{24,8},{1,17},{9,25},{17,1},{25,9},{2,18},{10... | collective-permute-start | bytes 3145736 | tf_op jit(solution)/shard_map/ppermute | solution.py:19
  126.7 46.2 %collective-permute-start = (bf16[2,256,1024]{2,1,0:T(8,128)(2,1)S(1)}, bf16[2,256,1024]{2,1,0:T(8,128)(2,1)S(1)}, u32[]{:S(2)}, u32[]{:S(2)}) collective-permute-start(bf16[2,256,1024]{2,1,0:T(8,128)(2,1)S(1)} %get-tuple-element.19), channel_id=1, source_target_pairs={{0,8},{8,16},{16,24},{24,0},{1,9},{9,17},{17,25},{25,1},{2,10},{10... | collective-permute-start | bytes 3145736 | tf_op jit(solution)/shard_map/ppermute | solution.py:19
Sparse Core Ops, SparseCore 0:
  9.0 61.0 all-gather.2

commit v3 on v2

--- a/solution.py
+++ b/solution.py
@@ -7,18 +7,11 @@
 from jax.experimental.pallas import tpu as pltpu
 from jax.sharding import PartitionSpec as P
 
-ROUNDS = 2
 TILE = 256
 VMEM_BYTES = 44 * 1024 * 1024
 MESH = pl.DeviceIdType.MESH
 
 
-def shifted(value, axis, steps):
-    count = lax.axis_size(axis)
-    pairs = [(source, (source + steps) % count) for source in range(count)]
-    return lax.ppermute(value, axis, pairs)
-
-
 def dot(left, right, left_dim=1, right_dim=0):
     return lax.dot_general(
         left, right, (((left_dim,), (right_dim,)), ((), ())), preferred_element_type=jnp.float32
@@ -27,6 +20,13 @@
 
 def low(value):
     return value.astype(jnp.bfloat16)
+
+
+def remote(source, target, send, recv, device):
+    return pltpu.make_async_remote_copy(
+        src_ref=source, dst_ref=target, send_sem=send, recv_sem=recv,
+        device_id=device, device_id_type=MESH,
+    )
 
 
 def gram_kernel(
@@ -46,12 +46,6 @@
     rows = [{"dp": lax.rem(row + s, n_dp), "mp": owner} for s in range(1, n_dp)]
     chips = [{"dp": row, "mp": lax.rem(chip + s, n_chips) * 2 + core} for s in range(1, n_chips)]
 
-    def remote(source, target, send, recv, device):
-        return pltpu.make_async_remote_copy(
-            src_ref=source, dst_ref=target, send_sem=send, recv_sem=recv,
-            device_id=device, device_id_type=MESH,
-        )
-
     barrier = pltpu.get_barrier_semaphore()
     for device in rows + chips + [sibling]:
         pl.semaphore_signal(barrier, inc=1, device_id=device, device_id_type=MESH)
@@ -65,7 +59,7 @@
         remote(o_ref, all_ref.at[own_tokens], o_send.at[s], o_recv.at[s], rows[s])
         for s in range(n_dp - 1)
     ]
-    for copy in f_copies + o_copies:
+    for copy in f_copies:
         copy.start()
     all_ref[own_tokens, :] = o_ref[...]
 
@@ -76,6 +70,9 @@
         slab[:, pl.ds(pl.multiple_of(source * tokens, tokens), tokens)] = dot(
             f_ref[...], others[s], 1, 1
         )
+
+    for copy in o_copies:
+        copy.start()
 
     theirs = pl.ds(pl.multiple_of((1 - core) * half, half), half)
     to_sibling = remote(slab.at[theirs], sibling_half, s_send, s_recv, sibling)
@@ -179,14 +176,55 @@
     return low(-0.5 * square + dot(low(second), low(tail)))
 
 
-def round_kernel(picked_ref, gram_ref, first_ref, second_ref, staying_ref, moving_ref, cross, upper, lower, side):
-    tokens = gram_ref.shape[0]
+def round_kernel(n_dp, n_mp, last, picked_ref, gram_ref, *refs):
+    if last:
+        (first_ref, second_ref, wide_ref, got_ref, staying_ref, arrived_ref, copy_ref, own_ref, *scratch) = refs
+        shift = 0
+    else:
+        first_ref, wide_ref, staying_ref, arrived_ref, copy_ref, *scratch = refs
+        second_ref = first_ref
+        shift = first_ref.shape[1] // 2
+    moving, cross, upper, lower, side, m_send, m_recv, x_send, x_recv = scratch
+    tokens, width = staying_ref.shape
+    row = lax.axis_index("dp")
+    owner = lax.axis_index("mp")
+    right = {"dp": row, "mp": lax.rem(owner + 1, n_mp)}
+    left = {"dp": row, "mp": lax.rem(owner + n_mp - 1, n_mp)}
+    greet = [right, left]
+    per = wide_ref.shape[0] // n_dp
+    rows = [{"dp": lax.rem(row + s, n_dp), "mp": owner} for s in range(1, n_dp)]
+    if not last:
+        greet = greet + rows
+
+    barrier = pltpu.get_barrier_semaphore()
+    for device in greet:
+        pl.semaphore_signal(barrier, inc=1, device_id=device, device_id_type=MESH)
+    pl.semaphore_wait(barrier, len(greet))
+
+    if last:
+        sibling = {"dp": row, "mp": owner + 1 - 2 * (owner % 2)}
+        exchange = [
+            remote(got_ref, copy_ref, x_send.at[0], x_recv.at[0], sibling),
+            remote(wide_ref.at[pl.ds(row * per, per)], own_ref, x_send.at[1], x_recv.at[1], sibling),
+        ]
+    else:
+        exchange = [
+            remote(
+                wide_ref.at[pl.ds(lax.rem(row + s + 1, n_dp) * per, per)], copy_ref.at[s],
+                x_send.at[s], x_recv.at[s], rows[s],
+            )
+            for s in range(n_dp - 1)
+        ]
+    for copy in exchange:
+        copy.start()
+
     cross[...] = jnp.zeros_like(cross)
 
     @pl.loop(0, tokens // TILE)
     def _(step):
         tile = pl.ds(pl.multiple_of(step * TILE, TILE), TILE)
-        cross[...] += dot(first_ref[tile, :], low(dot(gram_ref[tile, :], second_ref[...])), 0, 0)
+        product = low(dot(gram_ref[tile, :], second_ref[:, shift : shift + width]))
+        cross[...] += dot(first_ref[tile, :width], product, 0, 0)
 
     value = cross[...]
     scale = 0.5 * lax.rsqrt(jnp.sum(value * value) + 1e-06)
@@ -196,100 +234,121 @@
     side[...] = low(angle.astype(jnp.float32) + dot(upper[...], angle))
     keep = picked_ref[0] == 0
 
-    @pl.loop(0, tokens // TILE)
-    def _(step):
-        tile = pl.ds(pl.multiple_of(step * TILE, TILE), TILE)
-        first = first_ref[tile, :]
-        second = second_ref[tile, :]
+    travel = []
+    for step in range(tokens // TILE):
+        tile = pl.ds(step * TILE, TILE)
+        first = first_ref[tile, :width]
+        second = second_ref[tile, shift : shift + width]
         new_first = low(first.astype(jnp.float32) + (dot(first, upper[...]) - dot(second, side[...], 1, 1)))
         new_second = low(second.astype(jnp.float32) + (dot(first, side[...]) + dot(second, lower[...])))
-        moving_ref[tile, :] = jnp.where(keep, new_second, new_first)
+        moving[tile, :] = jnp.where(keep, new_second, new_first)
+        travel.append(remote(moving.at[tile], arrived_ref.at[tile], m_send.at[step], m_recv.at[step], right))
+        travel[-1].start()
         staying_ref[tile, :] = jnp.where(keep, new_first, new_second)
-
-
-def one_round(picked, gram, first, second, second_at):
+    for copy in travel + exchange:
+        copy.wait_recv()
+    for copy in travel + exchange:
+        copy.wait_send()
+
+
+def one_round(n_dp, n_mp, last, picked, gram, blocks, features):
     tokens = gram.shape[0]
-    width = second.shape[1] // (second_at + 1)
+    width = blocks[0].shape[1] // (1 if last else 2)
+    per = features[0].shape[0] // n_dp
+    depth = features[0].shape[1:]
+    tiles = tokens // TILE
     block = jax.ShapeDtypeStruct((tokens, width), jnp.bfloat16)
+    moved = [jax.ShapeDtypeStruct((n_dp - 1, per) + depth, jnp.bfloat16)]
+    if last:
+        moved.append(jax.ShapeDtypeStruct((per,) + depth, jnp.bfloat16))
+    copies = 2 if last else n_dp - 1
+    vmem = pl.BlockSpec(memory_space=pltpu.VMEM)
+    there = pl.BlockSpec(memory_space=pl.ANY)
+    square = pltpu.VMEM((width, width), jnp.bfloat16)
+    dma = pltpu.SemaphoreType.DMA
     return pl.pallas_call(
-        round_kernel,
-        grid=(1,),
-        out_shape=[block, block],
-        in_specs=[
-            pl.BlockSpec(memory_space=pltpu.SMEM),
-            pl.BlockSpec((tokens, tokens), lambda i: (0, 0)),
-            pl.BlockSpec((tokens, width), lambda i: (0, 0)),
-            pl.BlockSpec((tokens, width), lambda i: (0, second_at)),
+        functools.partial(round_kernel, n_dp, n_mp, last),
+        out_shape=[block, block] + moved,
+        in_specs=[pl.BlockSpec(memory_space=pltpu.SMEM), vmem] + [vmem] * len(blocks) + [there] * len(features),
+        out_specs=[vmem, vmem] + [there] * len(moved),
+        scratch_shapes=[
+            pltpu.VMEM((tokens, width), jnp.bfloat16),
+            pltpu.VMEM((width, width), jnp.float32),
+            square, square, square,
+            dma((tiles,)), dma((tiles,)), dma((copies,)), dma((copies,)),
         ],
-        out_specs=[pl.BlockSpec((tokens, width), lambda i: (0, 0))] * 2,
-        scratch_shapes=[
-            pltpu.VMEM((width, width), jnp.float32),
-            pltpu.VMEM((width, width), jnp.bfloat16),
-            pltpu.VMEM((width, width), jnp.bfloat16),
-            pltpu.VMEM((width, width), jnp.bfloat16),
-        ],
-        compiler_params=pltpu.CompilerParams(vmem_limit_bytes=VMEM_BYTES),
+        compiler_params=pltpu.CompilerParams(
+            collective_id=2 if last else 1, has_side_effects=True, vmem_limit_bytes=VMEM_BYTES
+        ),
         cost_estimate=pl.CostEstimate(
             flops=2 * tokens * width * (tokens + 5 * width) + 14 * width**3,
             bytes_accessed=2 * tokens * (tokens + 4 * width), transcendentals=1,
         ),
-        name="jacobi_round",
-    )(picked, gram, first, second)
+        name="jacobi_round_last" if last else "jacobi_round",
+    )(picked, gram, *blocks, *features)
 
 
 def product_kernel(n_dp, tokens, *refs):
-    parts = refs[:n_dp]
-    staying_ref, arrived_ref, out_ref = refs[n_dp:]
+    both = (refs[:n_dp], refs[n_dp : 2 * n_dp])
+    staying_ref, arrived_ref, out_ref = refs[2 * n_dp :]
     row = lax.axis_index("dp")
+    core = lax.axis_index("mp") % 2
     width = staying_ref.shape[1]
-    for side, block in enumerate((staying_ref, arrived_ref)):
-        total = None
-        for s in range(n_dp):
-            source = lax.rem(row + n_dp - s, n_dp)
-            term = dot(parts[s][0], block[pl.ds(pl.multiple_of(source * tokens, tokens), tokens), :], 0, 0)
-            total = term if total is None else total + term
-        out_ref[:, side * width : (side + 1) * width] = low(total)
-
-
-def final_product(parts, staying, arrived):
-    n_dp = len(parts)
-    groups, tokens, depth = parts[0].shape
+    for place, parts in enumerate(both):
+        where = core if place == 0 else 1 - core
+        for side, block in enumerate((staying_ref, arrived_ref)):
+            total = None
+            for s in range(n_dp):
+                source = lax.rem(row + n_dp - s, n_dp)
+                features = parts[s][...]
+                features = features.reshape(features.shape[-2:])
+                term = dot(features, block[pl.ds(pl.multiple_of(source * tokens, tokens), tokens), :], 0, 0)
+                total = term if total is None else total + term
+            out_ref[0, where, :, side * width : (side + 1) * width] = low(total)
+
+
+def final_product(mine, got, theirs, got_theirs, staying, arrived):
+    n_dp = got.shape[0] + 1
+    groups, tokens, depth = mine.shape
     tile = min(TILE, depth)
     per = depth // tile
     width = staying.shape[1]
     full = pl.BlockSpec(staying.shape, lambda i: (0, 0))
-    return pl.pallas_call(
+    own = pl.BlockSpec((1, tokens, tile), lambda i: (i // per, 0, i % per))
+
+    def other(s):
+        return pl.BlockSpec((1, 1, tokens, tile), lambda i: (s, i // per, 0, i % per))
+
+    others = [other(s) for s in range(n_dp - 1)]
+    out = pl.pallas_call(
         functools.partial(product_kernel, n_dp, tokens),
         grid=(groups * per,),
-        out_shape=jax.ShapeDtypeStruct((groups * depth, 2 * width), jnp.bfloat16),
-        in_specs=[pl.BlockSpec((1, tokens, tile), lambda i: (i // per, 0, i % per))] * n_dp + [full, full],
-        out_specs=pl.BlockSpec((tile, 2 * width), lambda i: (i, 0)),
+        out_shape=jax.ShapeDtypeStruct((groups, 2, depth, 2 * width), jnp.bfloat16),
+        in_specs=([own] + others) * 2 + [full, full],
+        out_specs=pl.BlockSpec((1, 2, tile, 2 * width), lambda i: (i // per, 0, i % per, 0)),
         compiler_params=pltpu.CompilerParams(vmem_limit_bytes=VMEM_BYTES),
         cost_estimate=pl.CostEstimate(
-            flops=4 * groups * depth * width * tokens * n_dp,
-            bytes_accessed=2 * groups * depth * (n_dp * tokens + 2 * width), transcendentals=0,
+            flops=8 * groups * depth * width * tokens * n_dp,
+            bytes_accessed=4 * groups * depth * (n_dp * tokens + 2 * width), transcendentals=0,
         ),
         name="final_product",
-    )(*parts, staying, arrived)
+    )(mine, *[got] * (n_dp - 1), theirs, *[got_theirs] * (n_dp - 1), staying, arrived)
+    return out.reshape(groups * 2 * depth, 2 * width)
 
 
 def on_device(features, out_grads, matching):
     n_dp = lax.axis_size("dp")
     n_mp = lax.axis_size("mp")
-    groups = n_mp // n_dp
-    row = lax.axis_index("dp")
-    wide = lax.all_gather(features, "mp", axis=0)
+    groups = n_mp // 2 // n_dp
+    same_core = [list(range(core, n_mp, 2)) for core in range(2)]
+    wide = lax.all_gather(features, "mp", axis=0, axis_index_groups=same_core)
     joined, gram = gather_and_gram(features, out_grads, n_dp, n_mp)
-    parts = []
-    for s in range(n_dp):
-        target = lax.rem(row + s, n_dp)
-        part = lax.dynamic_slice_in_dim(wide, target * groups, groups, axis=0)
-        parts.append(shifted(part, "dp", s) if s else part)
-    first, second, second_at = joined, joined, 1
-    for step in range(ROUNDS):
-        first, moving = one_round(matching[step], gram, first, second, second_at)
-        second, second_at = shifted(moving, "mp", 1), 0
-    return final_product(parts, first, second)
+    staying, arrived, got = one_round(n_dp, n_mp, False, matching[0], gram, [joined], [wide])
+    staying, arrived, got_theirs, theirs = one_round(
+        n_dp, n_mp, True, matching[1], gram, [staying, arrived], [wide, got]
+    )
+    mine = lax.dynamic_slice_in_dim(wide, lax.axis_index("dp") * groups, groups, axis=0)
+    return final_product(mine, got, theirs, got_theirs, staying, arrived)
 
 
 def solution(mesh):

time: 188 us -> 152 us (0.81)
  waiting for transfers between devices: 65 us -> 0.71 us
  Pallas kernels: 96.1 us -> 129 us
  starting transfers between devices: 2.9 us -> 0.01 us
    ppermute x5 -> x0, waiting for transfers between devices: 64.2 us -> none  [shifted(): return lax.ppermute(value, axis, pairs)]
    pallas_call x2, Pallas kernels: 18.6 us -> 53 us  [one_round(): pl.pallas_call(functools.partial(round_kernel, n_dp, n_mp, last), out_sha...]
    ppermute x5 -> x0, starting transfers between devices: 2.89 us -> none  [shifted(): return lax.ppermute(value, axis, pairs)]
  transfers between devices with their start and end apart: 6 -> 1, of which waited for: 4 -> 0; matrix products, arithmetic and copies ran while one was open for 2% -> 0% of each run, Pallas kernels for 47% -> 46%
where the time goes in v3:
time: 152 us; the launch traced here: 151 us
  Pallas kernels  129 us (85%)
  between operations  13.4 us (9%)
  local copies, waits for them, and re-layouts  8.2 us (5%)
    pallas_call x1, Pallas kernels, gather_and_gram(): pl.pallas_call(functools.partial(gram_kernel, n_dp, n_chips), out_shape=[...  68.9 us
    pallas_call x2, Pallas kernels, one_round(): pl.pallas_call(functools.partial(round_kernel, n_dp, n_mp, last), out_sha...  53 us
    pallas_call x1, Pallas kernels, final_product(): pl.pallas_call(functools.partial(product_kernel, n_dp, tokens), grid=(gro...  6.95 us
    unnamed x12, local copies, waits for them, and re-layouts  6.57 us
  transfers between devices with their start and end apart: 1, of which 0 were waited for; matrix products, arithmetic and copies ran while one was open for 0% of the time, Pallas kernels for 46%

profile of v3, /device:TPU:0, one launch (start us, length us, event | category | flops | bytes accessed | tf_op | source)
XLA Modules:
  0.0 151.3 jit_solution(8272834606152206322)
XLA Ops:
  6.5 0.0 copy-start.5
  6.5 0.0 all-gather.3.cloned.1.call-start
  6.5 0.7 all-gather.3.cloned.1.call-update
  7.3 0.0 copy-start
  7.3 1.0 copy-done
  8.3 0.0 copy-start.2
  8.3 1.0 copy-done.2
  9.3 68.9 %gather_and_gram.1 = (bf16[1024,1024]{1,0:T(8,128)(2,1)S(1)}, bf16[1024,1024]{1,0:T(8,128)(2,1)S(1)}) custom-call(bf16[256,1024]{1,0:T(8,128)(2,1)S(1)} %copy-done, bf16[256,1024]{1,0:T(8,128)(2,1)S(1)} %copy-done.2), custom_call_target="tpu_custom_call" | custom-call | flops 536870912 | bytes 200000000 | tf_op jit(solution)/shard_map/gather_and_gram/pallas_call | solution.py:144
  78.3 0.0 copy-start.3
  78.3 1.3 copy-done.3
  79.6 0.0 copy-done.5
  79.6 0.6 fusion
  80.2 0.0 all-gather.3.cloned.1.call-done
  80.2 1.1 constant_dynamic-slice_fusion.refs_0_
  81.3 0.0 copy-start.1
  81.3 1.6 %copy-done.1 = bf16[1024,1024]{1,0:T(8,128)(2,1)S(1)} copy-done((bf16[1024,1024]{1,0:T(8,128)(2,1)S(1)}, bf16[1024,1024]{1,0:T(8,128)(2,1)}, u32[]{:S(2)}) %copy-start.1) | copy-done | bytes 2097176
  82.9 0.0 copy-start.4
  82.9 1.6 %copy-done.4 = bf16[1024,1024]{1,0:T(8,128)(2,1)S(1)} copy-done((bf16[1024,1024]{1,0:T(8,128)(2,1)S(1)}, bf16[1024,1024]{1,0:T(8,128)(2,1)}, u32[]{:S(2)}) %copy-start.4) | copy-done | bytes 2097176
  84.4 30.0 %jacobi_round.1 = (bf16[1024,512]{1,0:T(8,128)(2,1)S(1)}, bf16[1024,512]{1,0:T(8,128)(2,1)S(1)}, bf16[3,1,256,1024]{3,2,1,0:T(8,128)(2,1)S(1)}) custom-call(s32[1]{0:T(128)} %bitcast.1.picked_ref, bf16[1024,1024]{1,0:T(8,128)(2,1)S(1)} %get-tuple-element.14.gram_ref, bf16[1024,1024]{1,0:T(8,128)(2,1)S(1)} %copy-done.4, bf16[4,256,1024]{2,1,0:T(8,128)(2,1)S(1)} %bitcast.6), custom_call_target="tpu_custom_call" | custom-call | flops 5637144576 | bytes 6291456 | tf_op jit(solution)/shard_map/jacobi_round/pallas_call | solution.py:269
  114.4 23.0 %jacobi_round_last.1 = (bf16[1024,512]{1,0:T(8,128)(2,1)S(1)}, bf16[1024,512]{1,0:T(8,128)(2,1)S(1)}, bf16[3,1,256,1024]{3,2,1,0:T(8,128)(2,1)S(1)}, bf16[1,256,1024]{2,1,0:T(8,128)(2,1)S(1)}) custom-call(s32[1]{0:T(128)} %bitcast.2.picked_ref, bf16[1024,1024]{1,0:T(8,128)(2,1)S(1)} %get-tuple-element.14.gram_ref, ...), custom_call_target="tpu_custom_call" | custom-call | flops 5637144576 | bytes 6291456 | tf_op jit(solution)/shard_map/jacobi_round_last/pallas_call | solution.py:269
  137.5 6.9 %final_product.1 = bf16[1,2,1024,1024]{3,2,1,0:T(8,128)(2,1)} custom-call(bf16[1,256,1024]{2,1,0:T(8,128)(2,1)S(1)} %constant_dynamic-slice_fusion.refs_0_, bf16[3,1,256,1024]{3,2,1,0:T(8,128)(2,1)S(1)} %get-tuple-element.16.refs_3_.refs_1_.refs_2_, bf16[3,1,256,1024]{3,2,1,0:T(8,128)(2,1)S(1)} %get-tuple-element.16.refs_3_.refs_1_.refs_2_, ...), custom_call_target="tpu_custom_call" | custom-call | flops 4294967296 | bytes 8388608 | tf_op jit(solution)/shard_map/final_product/pallas_call | solution.py:323
Async XLA Ops:
  6.5 73.1 %copy-start.5 = (s32[2,1]{0,1:T(1,128)S(1)}, s32[2,1]{0,1:T(1,128)}, u32[]{:S(2)}) copy-start(s32[2,1]{0,1:T(1,128)} %param.5) | copy-start | bytes 28
  6.5 73.6 %all-gather.3.cloned.1.call-start = ((), (), s32[]{:S(2)}) async-start(), calls=%async_computation | async-start | bytes 2621440 | tf_op jit(solution)/shard_map/all_gather | solution.py:344
  7.3 1.0 copy-start
  8.3 1.0 copy-start.2
  78.3 1.3 copy-start.3
  81.3 1.6 %copy-start.1 = (bf16[1024,1024]{1,0:T(8,128)(2,1)S(1)}, bf16[1024,1024]{1,0:T(8,128)(2,1)}, u32[]{:S(2)}) copy-start(bf16[1024,1024]{1,0:T(8,128)(2,1)} %all-gather.3.cloned.1.call-done) | copy-start | bytes 6291460
  82.9 1.6 %copy-start.4 = (bf16[1024,1024]{1,0:T(8,128)(2,1)S(1)}, bf16[1024,1024]{1,0:T(8,128)(2,1)}, u32[]{:S(2)}) copy-start(bf16[1024,1024]{1,0:T(8,128)(2,1)} %copy-done.3) | copy-start | bytes 6291460
Sparse Core Ops, SparseCore 0:
  8.9 59.7 all-gather.2

commit v4 on v3

--- a/solution.py
+++ b/solution.py
@@ -30,10 +30,10 @@
 
 
 def gram_kernel(
-    n_dp, n_chips, f_ref, o_ref, all_ref, gram_ref,
-    others, slab, sibling_half, out_half, chip_in,
+    n_dp, n_chips, picked_ref, f_ref, o_ref, staying_ref, arrived_ref, gram_ref,
+    all_ref, others, slab, sibling_half, out_half, chip_in,
     f_send, f_recv, o_send, o_recv, s_send, s_recv, z_send, z_recv,
-    a_send, a_recv, b_send, b_recv, c_send, c_recv,
+    a_send, a_recv, b_send, b_recv, c_send, c_recv, *scratch,
 ):
     tokens = f_ref.shape[0]
     half = tokens // 2
@@ -47,9 +47,11 @@
     chips = [{"dp": row, "mp": lax.rem(chip + s, n_chips) * 2 + core} for s in range(1, n_chips)]
 
     barrier = pltpu.get_barrier_semaphore()
-    for device in rows + chips + [sibling]:
+    right = {"dp": row, "mp": lax.rem(owner + 1, 2 * n_chips)}
+    left = {"dp": row, "mp": lax.rem(owner + 2 * n_chips - 1, 2 * n_chips)}
+    for device in rows + chips + [right, left]:
         pl.semaphore_signal(barrier, inc=1, device_id=device, device_id_type=MESH)
-    pl.semaphore_wait(barrier, n_dp + n_chips - 1)
+    pl.semaphore_wait(barrier, n_dp + n_chips)
 
     f_copies = [
         remote(f_ref, others.at[s], f_send.at[s], f_recv.at[s], rows[s]) for s in range(n_dp - 1)
@@ -128,41 +130,58 @@
         c_copies[-1].start()
     for copy in c_copies + o_copies:
         copy.wait_recv()
-    for copy in f_copies + o_copies + [to_sibling] + z_copies + a_copies + b_copies + c_copies:
+    travel = jacobi_round(
+        picked_ref, gram_ref, all_ref, all_ref, all_ref.shape[1] // 2, staying_ref, arrived_ref, right, *scratch
+    )
+    for copy in travel:
+        copy.wait_recv()
+    for copy in f_copies + o_copies + [to_sibling] + z_copies + a_copies + b_copies + c_copies + travel:
         copy.wait_send()
 
 
-def gather_and_gram(features, out_grads, n_dp, n_mp):
+def round_scratch(every, width):
+    square = pltpu.VMEM((width, width), jnp.bfloat16)
+    tiles = pltpu.SemaphoreType.DMA((every // TILE,))
+    return [
+        pltpu.VMEM((every, width), jnp.bfloat16), pltpu.VMEM((width, width), jnp.float32),
+        square, square, square, tiles, tiles,
+    ]
+
+
+def gather_and_round(picked, features, out_grads, n_dp, n_mp):
     tokens, depth = features.shape
     every = n_dp * tokens
     n_chips = n_mp // 2
     half = tokens // 2
+    width = out_grads.shape[1] // 2
     dma = pltpu.SemaphoreType.DMA
     peers = [dma((n_dp - 1,))] * 2
     around = [dma((n_chips - 1,))] * 2
     whole = pl.BlockSpec(memory_space=pltpu.VMEM)
+    block = jax.ShapeDtypeStruct((every, width), jnp.bfloat16)
     return pl.pallas_call(
         functools.partial(gram_kernel, n_dp, n_chips),
-        out_shape=[
-            jax.ShapeDtypeStruct((every, out_grads.shape[1]), jnp.bfloat16),
-            jax.ShapeDtypeStruct((every, every), jnp.bfloat16),
-        ],
-        in_specs=[whole, whole],
-        out_specs=[whole, whole],
+        out_shape=[block, block, jax.ShapeDtypeStruct((every, every), jnp.bfloat16)],
+        in_specs=[pl.BlockSpec(memory_space=pltpu.SMEM), whole, whole],
+        out_specs=[whole, whole, whole],
         scratch_shapes=[
+            pltpu.VMEM((every, 2 * width), jnp.bfloat16),
             pltpu.VMEM((n_dp - 1, tokens, depth), jnp.bfloat16),
             pltpu.VMEM((tokens, every), jnp.float32),
             pltpu.VMEM((half, every), jnp.float32),
             pltpu.VMEM((half, every), jnp.bfloat16),
             pltpu.VMEM((n_chips - 1, half // n_chips, every), jnp.bfloat16),
         ]
-        + peers + peers + [dma, dma] + around + around + peers + [dma((n_dp,))] * 2,
+        + peers + peers + [dma, dma] + around + around + peers + [dma((n_dp,))] * 2
+        + round_scratch(every, width),
         compiler_params=pltpu.CompilerParams(
             collective_id=0, has_side_effects=True, vmem_limit_bytes=VMEM_BYTES
         ),
-        cost_estimate=pl.CostEstimate(flops=2 * tokens * every * depth, bytes_accessed=200_000_000, transcendentals=0),
-        name="gather_and_gram",
-    )(features, out_grads)
+        cost_estimate=pl.CostEstimate(
+            flops=2 * tokens * every * depth, bytes_accessed=250_000_000, transcendentals=0
+        ),
+        name="gather_and_round",
+    )(picked, features, out_grads)
 
 
 def even_part(square):
@@ -176,48 +195,11 @@
     return low(-0.5 * square + dot(low(second), low(tail)))
 
 
-def round_kernel(n_dp, n_mp, last, picked_ref, gram_ref, *refs):
-    if last:
-        (first_ref, second_ref, wide_ref, got_ref, staying_ref, arrived_ref, copy_ref, own_ref, *scratch) = refs
-        shift = 0
-    else:
-        first_ref, wide_ref, staying_ref, arrived_ref, copy_ref, *scratch = refs
-        second_ref = first_ref
-        shift = first_ref.shape[1] // 2
-    moving, cross, upper, lower, side, m_send, m_recv, x_send, x_recv = scratch
+def jacobi_round(
+    picked_ref, gram_ref, first_ref, second_ref, shift, staying_ref, arrived_ref, right,
+    moving, cross, upper, lower, side, m_send, m_recv,
+):
     tokens, width = staying_ref.shape
-    row = lax.axis_index("dp")
-    owner = lax.axis_index("mp")
-    right = {"dp": row, "mp": lax.rem(owner + 1, n_mp)}
-    left = {"dp": row, "mp": lax.rem(owner + n_mp - 1, n_mp)}
-    greet = [right, left]
-    per = wide_ref.shape[0] // n_dp
-    rows = [{"dp": lax.rem(row + s, n_dp), "mp": owner} for s in range(1, n_dp)]
-    if not last:
-        greet = greet + rows
-
-    barrier = pltpu.get_barrier_semaphore()
-    for device in greet:
-        pl.semaphore_signal(barrier, inc=1, device_id=device, device_id_type=MESH)
-    pl.semaphore_wait(barrier, len(greet))
-
-    if last:
-        sibling = {"dp": row, "mp": owner + 1 - 2 * (owner % 2)}
-        exchange = [
-            remote(got_ref, copy_ref, x_send.at[0], x_recv.at[0], sibling),
-            remote(wide_ref.at[pl.ds(row * per, per)], own_ref, x_send.at[1], x_recv.at[1], sibling),
-        ]
-    else:
-        exchange = [
-            remote(
-                wide_ref.at[pl.ds(lax.rem(row + s + 1, n_dp) * per, per)], copy_ref.at[s],
-                x_send.at[s], x_recv.at[s], rows[s],
-            )
-            for s in range(n_dp - 1)
-        ]
-    for copy in exchange:
-        copy.start()
-
     cross[...] = jnp.zeros_like(cross)
 
     @pl.loop(0, tokens // TILE)
@@ -245,47 +227,77 @@
         travel.append(remote(moving.at[tile], arrived_ref.at[tile], m_send.at[step], m_recv.at[step], right))
         travel[-1].start()
         staying_ref[tile, :] = jnp.where(keep, new_first, new_second)
-    for copy in travel + exchange:
+    return travel
+
+
+def last_kernel(
+    n_dp, n_mp, picked_ref, gram_ref, first_ref, second_ref, wide_ref,
+    staying_ref, arrived_ref, got_ref, got_theirs_ref, theirs_ref,
+    x_send, x_recv, y_send, y_recv, *scratch,
+):
+    row = lax.axis_index("dp")
+    owner = lax.axis_index("mp")
+    right = {"dp": row, "mp": lax.rem(owner + 1, n_mp)}
+    left = {"dp": row, "mp": lax.rem(owner + n_mp - 1, n_mp)}
+    sibling = {"dp": row, "mp": owner + 1 - 2 * (owner % 2)}
+    per = wide_ref.shape[0] // n_dp
+    rows = [{"dp": lax.rem(row + s, n_dp), "mp": owner} for s in range(1, n_dp)]
+
+    barrier = pltpu.get_barrier_semaphore()
+    for device in [right, left] + rows:
+        pl.semaphore_signal(barrier, inc=1, device_id=device, device_id_type=MESH)
+    pl.semaphore_wait(barrier, n_dp + 1)
+
+    exchange = [
+        remote(
+            wide_ref.at[pl.ds(lax.rem(row + s + 1, n_dp) * per, per)], got_ref.at[s],
+            x_send.at[s], x_recv.at[s], rows[s],
+        )
+        for s in range(n_dp - 1)
+    ]
+    across = [
+        remote(wide_ref.at[pl.ds(row * per, per)], theirs_ref, y_send.at[n_dp - 1], y_recv.at[n_dp - 1], sibling)
+    ]
+    for copy in exchange + across:
+        copy.start()
+    travel = jacobi_round(
+        picked_ref, gram_ref, first_ref, second_ref, 0, staying_ref, arrived_ref, right, *scratch
+    )
+    for s in range(n_dp - 1):
+        exchange[s].wait_recv()
+        across.append(remote(got_ref.at[s], got_theirs_ref.at[s], y_send.at[s], y_recv.at[s], sibling))
+        across[-1].start()
+    for copy in travel + across:
         copy.wait_recv()
-    for copy in travel + exchange:
+    for copy in travel + exchange + across:
         copy.wait_send()
 
 
-def one_round(n_dp, n_mp, last, picked, gram, blocks, features):
-    tokens = gram.shape[0]
-    width = blocks[0].shape[1] // (1 if last else 2)
-    per = features[0].shape[0] // n_dp
-    depth = features[0].shape[1:]
-    tiles = tokens // TILE
-    block = jax.ShapeDtypeStruct((tokens, width), jnp.bfloat16)
-    moved = [jax.ShapeDtypeStruct((n_dp - 1, per) + depth, jnp.bfloat16)]
-    if last:
-        moved.append(jax.ShapeDtypeStruct((per,) + depth, jnp.bfloat16))
-    copies = 2 if last else n_dp - 1
+def last_round(n_dp, n_mp, picked, gram, first, second, wide):
+    every, width = first.shape
+    per = wide.shape[0] // n_dp
+    depth = wide.shape[1:]
+    block = jax.ShapeDtypeStruct((every, width), jnp.bfloat16)
+    moved = jax.ShapeDtypeStruct((n_dp - 1, per) + depth, jnp.bfloat16)
     vmem = pl.BlockSpec(memory_space=pltpu.VMEM)
     there = pl.BlockSpec(memory_space=pl.ANY)
-    square = pltpu.VMEM((width, width), jnp.bfloat16)
     dma = pltpu.SemaphoreType.DMA
     return pl.pallas_call(
-        functools.partial(round_kernel, n_dp, n_mp, last),
-        out_shape=[block, block] + moved,
-        in_specs=[pl.BlockSpec(memory_space=pltpu.SMEM), vmem] + [vmem] * len(blocks) + [there] * len(features),
-        out_specs=[vmem, vmem] + [there] * len(moved),
-        scratch_shapes=[
-            pltpu.VMEM((tokens, width), jnp.bfloat16),
-            pltpu.VMEM((width, width), jnp.float32),
-            square, square, square,
-            dma((tiles,)), dma((tiles,)), dma((copies,)), dma((copies,)),
-        ],
+        functools.partial(last_kernel, n_dp, n_mp),
+        out_shape=[block, block, moved, moved, jax.ShapeDtypeStruct((per,) + depth, jnp.bfloat16)],
+        in_specs=[pl.BlockSpec(memory_space=pltpu.SMEM), vmem, vmem, vmem, there],
+        out_specs=[vmem, vmem, there, there, there],
+        scratch_shapes=[dma((n_dp - 1,)), dma((n_dp - 1,)), dma((n_dp,)), dma((n_dp,))]
+        + round_scratch(every, width),
         compiler_params=pltpu.CompilerParams(
-            collective_id=2 if last else 1, has_side_effects=True, vmem_limit_bytes=VMEM_BYTES
+            collective_id=1, has_side_effects=True, vmem_limit_bytes=VMEM_BYTES
         ),
         cost_estimate=pl.CostEstimate(
-            flops=2 * tokens * width * (tokens + 5 * width) + 14 * width**3,
-            bytes_accessed=2 * tokens * (tokens + 4 * width), transcendentals=1,
-        ),
-        name="jacobi_round_last" if last else "jacobi_round",
-    )(picked, gram, *blocks, *features)
+            flops=2 * every * width * (every + 5 * width) + 14 * width**3,
+            bytes_accessed=2 * every * (every + 4 * width), transcendentals=1,
+        ),
+        name="last_round",
+    )(picked, gram, first, second, wide)
 
 
 def product_kernel(n_dp, tokens, *refs):
@@ -342,10 +354,9 @@
     groups = n_mp // 2 // n_dp
     same_core = [list(range(core, n_mp, 2)) for core in range(2)]
     wide = lax.all_gather(features, "mp", axis=0, axis_index_groups=same_core)
-    joined, gram = gather_and_gram(features, out_grads, n_dp, n_mp)
-    staying, arrived, got = one_round(n_dp, n_mp, False, matching[0], gram, [joined], [wide])
-    staying, arrived, got_theirs, theirs = one_round(
-        n_dp, n_mp, True, matching[1], gram, [staying, arrived], [wide, got]
+    staying, arrived, gram = gather_and_round(matching[0], features, out_grads, n_dp, n_mp)
+    staying, arrived, got, got_theirs, theirs = last_round(
+        n_dp, n_mp, matching[1], gram, staying, arrived, wide
     )
     mine = lax.dynamic_slice_in_dim(wide, lax.axis_index("dp") * groups, groups, axis=0)
     return final_product(mine, got, theirs, got_theirs, staying, arrived)

time: 152 us -> 150 us (0.987)
    unnamed x12 -> x8, local copies, waits for them, and re-layouts: 6.57 us -> 4.27 us
    pallas_call x3 -> x2, Pallas kernels: 122 us -> 121 us  [the longest x1 93.2 us: gather_and_round(): pl.pallas_call(functools.partial(gram_kernel, n_dp, n_chips), out_shape=[...]
  transfers between devices with their start and end apart: 1 -> 1, of which waited for: 0 -> 0; matrix products, arithmetic and copies ran while one was open for 0% -> 1% of each run, Pallas kernels for 46% -> 62%
where the time goes in v4:
time: 150 us; the launch traced here: 149 us
  Pallas kernels  128 us (85%)
  between operations  13.4 us (9%)
  local copies, waits for them, and re-layouts  6.71 us (4%)
    pallas_call x1, Pallas kernels, gather_and_round(): pl.pallas_call(functools.partial(gram_kernel, n_dp, n_chips), out_shape=[...  93.2 us
    pallas_call x1, Pallas kernels, last_round(): pl.pallas_call(functools.partial(last_kernel, n_dp, n_mp), out_shape=[blo...  28.2 us
    pallas_call x1, Pallas kernels, final_product(): pl.pallas_call(functools.partial(product_kernel, n_dp, tokens), grid=(gro...  6.95 us
    unnamed x8, local copies, waits for them, and re-layouts  4.27 us
  transfers between devices with their start and end apart: 1, of which 0 were waited for; matrix products, arithmetic and copies ran while one was open for 1% of the time, Pallas kernels for 62%

profile of v4, /device:TPU:0, one launch (start us, length us, event | category | flops | bytes accessed | tf_op | source)
XLA Modules:
  0.0 149.2 jit_solution(1395192421625207846)
XLA Ops:
  6.5 0.0 all-gather.3.cloned.1.call-start
  6.5 0.7 all-gather.3.cloned.1.call-update
  7.3 1.4 fusion
  8.6 0.0 copy-start
  8.6 1.0 copy-done
  9.7 0.0 copy-start.1
  9.7 1.0 copy-done.1
  10.7 93.2 %gather_and_round.1 = (bf16[1024,512]{1,0:T(8,128)(2,1)S(1)}, bf16[1024,512]{1,0:T(8,128)(2,1)S(1)}, bf16[1024,1024]{1,0:T(8,128)(2,1)S(1)}) custom-call(s32[1]{0:T(128)} %bitcast.2.picked_ref, bf16[256,1024]{1,0:T(8,128)(2,1)S(1)} %copy-done, bf16[256,1024]{1,0:T(8,128)(2,1)S(1)} %copy-done.1), custom_call_target="tpu_custom_call" | custom-call | flops 536870912 | bytes 250000000 | tf_op jit(solution)/shard_map/gather_and_round/pallas_call | solution.py:162
  103.9 0.0 copy-start.2
  103.9 1.0 copy-done.2
  104.9 0.0 all-gather.3.cloned.1.call-done
  104.9 1.1 constant_dynamic-slice_fusion.refs_0_
  105.9 0.0 copy-start.3
  106.0 1.2 copy-done.3
  107.2 28.2 %last_round.1 = (bf16[1024,512]{1,0:T(8,128)(2,1)S(1)}, bf16[1024,512]{1,0:T(8,128)(2,1)S(1)}, bf16[3,1,256,1024]{3,2,1,0:T(8,128)(2,1)S(1)}, bf16[3,1,256,1024]...) custom-call(s32[1]{0:T(128)} %bitcast.1.picked_ref, bf16[1024,1024]{1,0:T(8,128)(2,1)S(1)} %get-tuple-element.13.gram_ref, ...), custom_call_target="tpu_custom_call" | custom-call | flops 5637144576 | bytes 6291456 | tf_op jit(solution)/shard_map/last_round/pallas_call | solution.py:285
  135.4 7.0 %final_product.1 = bf16[1,2,1024,1024]{3,2,1,0:T(8,128)(2,1)} custom-call(bf16[1,256,1024]{2,1,0:T(8,128)(2,1)S(1)} %constant_dynamic-slice_fusion.refs_0_, bf16[3,1,256,1024]{3,2,1,0:T(8,128)(2,1)S(1)} %get-tuple-element.16.refs_1_.refs_2_.refs_3_, bf16[3,1,256,1024]{3,2,1,0:T(8,128)(2,1)S(1)} %get-tuple-element.16.refs_1_.refs_2_.refs_3_, ...), custom_call_target="tpu_custom_call" | custom-call | flops 4294967296 | bytes 8388608 | tf_op jit(solution)/shard_map/final_product/pallas_call | solution.py:335
Async XLA Ops:
  6.5 98.3 %all-gather.3.cloned.1.call-start = ((), (), s32[]{:S(2)}) async-start(), calls=%async_computation | async-start | bytes 2621440 | tf_op jit(solution)/shard_map/all_gather | solution.py:356
  8.6 1.0 copy-start
  9.7 1.0 copy-start.1
  103.9 1.0 copy-start.2
  105.9 1.2 copy-start.3
Sparse Core Ops, SparseCore 0:
  8.9 59.8 all-gather.2
